TPU v7x, 256 devices: a whole 4x4x8 slice. The times are simulated.
256 devices in a mesh: row: 16 (over y, z_lo), col: 16 (over x, z_hi, core).
Axes of the slice: x: 4, y: 4, z: 8 (z_hi: 2, z_lo: 4; z = z_hi * 4 + z_lo), core: 2. Of those that a mesh axis runs over, the one named last changes fastest.
Arguments:
- momentum: bfloat16 [5376, 10240], P('row', 'col'), may hold values from -6 to 6
Outputs:
- update: bfloat16 [5376, 10240], P('row', 'col')
All inputs are finite; a program needn't handle non-finite values.
Results may differ from a plain program's by a relative error of at most 0.0059.
Values may be sent and summed in bfloat16 or wider, within the bound.
No kernel may reach another device: no remote copies, remote signals or barrier semaphores. Data moves between devices by JAX's collectives and lax.ppermute only.
A program may use at most 64 MiB of HBM per device.

v0:
```python
import jax
import jax.numpy as jnp
from jax import lax
from jax.sharding import Mesh, PartitionSpec as P

C = 10240
B = 336
H = 168
CUT = 512

coef_a = 3.4445
coef_b = -4.775
coef_c = 2.0315

AXES = ("y", "zl", "x", "zh", "core")
OFFSETS = (1, 2, 3)


def send_xor(v, axis, size, k):
    return lax.ppermute(v, axis, [(i, i ^ k) for i in range(size)])


def send_up(v, axis, size, k):
    return lax.ppermute(v, axis, [(i, (i + k) % size) for i in range(size)])


def wide(v):
    return v.astype(jnp.float32)


def narrow(v):
    return v.astype(jnp.bfloat16)


def dot(a, b, da, db):
    return lax.dot_general(a, b, (((da,), (db,)), ((), ())), preferred_element_type=jnp.float32)


def swap(v):
    return send_xor(v, "core", 2, 1)


def pick(core, v):
    return jnp.where(core == 0, v[:H], v[H:])


SLOT_A = [(1, 0), (3, 1), (0, 2), (2, 3)]
SLOT_B = [(3, 0), (1, 2)]


def fetch_z(v):
    return [lax.ppermute(v, "zl", SLOT_A), lax.ppermute(v, "zl", SLOT_B)]


def fetch_y(v):
    return [send_up(v, "y", 4, -s) for s in OFFSETS]


def apply_gram(gram, columns, rows):
    part = dot(gram, columns, 1, 0)
    back = narrow(dot(gram[:, : 2 * B], rows, 0, 0))
    sent = narrow(part)
    total = part[:B]
    total = total + wide(lax.ppermute(back[:B], "zl", [(b, a) for a, b in SLOT_A]))
    total = total + wide(lax.ppermute(back[B:], "zl", [(b, a) for a, b in SLOT_B]))
    for s in OFFSETS:
        total = total + wide(send_up(sent[s * B : (s + 1) * B], "y", 4, s))
    return total


def sum_x(chip, xi):
    total = wide(lax.dynamic_index_in_dim(chip, xi, 0, keepdims=False))
    for k in OFFSETS:
        piece = lax.dynamic_index_in_dim(chip, xi ^ k, 0, keepdims=False)
        total = total + wide(send_xor(piece, "x", 4, k))
    return total


def gram_chunk(total, xi):
    total = total + wide(send_xor(narrow(total), "zh", 2, 1))
    mine = narrow(total / C)
    rows = jnp.zeros((4,) + mine.shape, jnp.bfloat16)
    rows = lax.dynamic_update_index_in_dim(rows, mine, xi, 0)
    for k in OFFSETS:
        rows = lax.dynamic_update_index_in_dim(rows, send_xor(mine, "x", 4, k), xi ^ k, 0)
    return rows, swap(rows)


def body(momentum):
    core = lax.axis_index("core")
    xi = lax.axis_index("x")
    za, zb = fetch_z(momentum)
    y = fetch_y(momentum)
    m_o = swap(momentum)
    rows = [jnp.concatenate([pick(core, momentum), pick(core, m_o)], axis=1)]
    rows += [jnp.concatenate([pick(core, v), swap(pick(1 - core, v))], axis=1) for v in y]
    rows = jnp.concatenate(rows, axis=0)
    za_w, zb_w, own_w = (
        jnp.concatenate([v, o], axis=1)
        for v, o in ((za, swap(za)), (zb, swap(zb)), (momentum, m_o))
    )

    def chip_chunk(blocks):
        columns = jnp.concatenate(blocks, axis=0)
        return narrow(dot(rows, columns, 1, 1)).reshape(4, H, columns.shape[0])

    cut = CUT - B
    sum_a = sum_x(chip_chunk([za_w, zb_w[:cut]]), xi)
    sum_b = sum_x(chip_chunk([zb_w[cut:], own_w]), xi)
    gram = jnp.zeros((4, 2, H, 3 * B), jnp.bfloat16)
    for total, place in ((sum_a, 0), (sum_b, CUT)):
        part, other = gram_chunk(total, xi)
        gram = lax.dynamic_update_slice(gram, part[:, None], (0, core, 0, place))
        gram = lax.dynamic_update_slice(gram, other[:, None], (0, 1 - core, 0, place))
    gram = gram.reshape(4 * B, 3 * B)
    columns = jnp.concatenate([za, zb, momentum], axis=0)
    first = apply_gram(gram, columns, jnp.concatenate([momentum] + y, axis=0))
    sent = narrow(first)
    columns = jnp.concatenate(fetch_z(sent) + [sent], axis=0)
    second = apply_gram(gram, columns, jnp.concatenate([sent] + fetch_y(sent), axis=0))
    return narrow(coef_a * wide(momentum) + coef_b * first + coef_c * second)


def solution(mesh):
    fine = Mesh(mesh.devices.reshape(4, 4, 4, 2, 2), AXES)
    spec = P(("y", "zl"), ("x", "zh", "core"))
    return jax.shard_map(body, mesh=fine, in_specs=(spec,), out_specs=spec, check_vma=False)
```

profile of v0, /device:TPU:1, one launch (start us, length us, event | category | flops | bytes accessed | tf_op | source)
XLA Modules:
  0.0 166.7 jit_solution(432880720247602997)
XLA Ops:
  3.4 3.1 %collective-permute-start.7 = (bf16[336,640]{1,0:T(8,128)(2,1)}, bf16[336,640]{1,0:T(8,128)(2,1)S(1)}, u32[]{:S(2)}, u32[]{:S(2)}) collective-permute-start(bf16[336,640]{1,0:T(8,128)(2,1)} %param.1), channel_id=1, source_target_pairs={{16,0},{48,16},{0,32},{32,48},{17,1},{49,17},{1,33},{33,49},{18,2}... | collective-permute-start | bytes 1290248 | tf_op jit(solution)/shard_map/ppermute | solution.py:52
  6.5 2.6 %collective-permute-start.3 = (bf16[336,640]{1,0:T(8,128)(2,1)}, bf16[336,640]{1,0:T(8,128)(2,1)S(1)}, u32[]{:S(2)}, u32[]{:S(2)}) collective-permute-start(bf16[336,640]{1,0:T(8,128)(2,1)} %param.1), channel_id=1, source_target_pairs={{0,128},{64,192},{128,0},{192,64},{1,129},{65,193},{129,1},{193,65... | collective-permute-start | bytes 1290248 | tf_op jit(solution)/shard_map/ppermute | solution.py:24
  11.4 3.3 %collective-permute-start = (bf16[336,640]{1,0:T(8,128)(2,1)}, bf16[336,640]{1,0:T(8,128)(2,1)S(1)}, u32[]{:S(2)}, u32[]{:S(2)}) collective-permute-start(bf16[336,640]{1,0:T(8,128)(2,1)} %param.1), channel_id=1, source_target_pairs={{0,1},{1,0},{2,3},{3,2},{4,5},{5,4},{6,7},{7,6},{8,9},{9,8},{10,11... | collective-permute-start | bytes 1290248 | tf_op jit(solution)/shard_map/ppermute | solution.py:20
  14.7 8.8 %collective-permute-done.3 = bf16[336,640]{1,0:T(8,128)(2,1)S(1)} collective-permute-done((bf16[336,640]{1,0:T(8,128)(2,1)}, bf16[336,640]{1,0:T(8,128)(2,1)S(1)}, u32[]{:S(2)}, u32[]{:S(2)}) %collective-permute-start.3) | collective-permute-done | bytes 430112 | tf_op jit(solution)/shard_map/ppermute | solution.py:24
  25.2 2.2 %collective-permute-done.1 = bf16[336,640]{1,0:T(8,128)(2,1)S(1)} collective-permute-done((bf16[336,640]{1,0:T(8,128)(2,1)}, bf16[336,640]{1,0:T(8,128)(2,1)S(1)}, u32[]{:S(2)}, u32[]{:S(2)}) %collective-permute-start.1) | collective-permute-done | bytes 430112 | tf_op jit(solution)/shard_map/ppermute | solution.py:24
  40.9 2.4 %collective-permute-done.20 = bf16[168,496]{1,0:T(8,128)(2,1)S(1)} collective-permute-done((bf16[168,496]{1,0:T(8,128)(2,1)S(1)}, bf16[168,496]{1,0:T(8,128)(2,1)S(1)}, u32[]{:S(2)}, u32[]{:S(2)}) %collective-permute-start.20) | collective-permute-done | bytes 166688 | tf_op jit(solution)/shard_map/ppermute | solution.py:20
  43.4 5.2 %collective-permute-start.22 = (bf16[168,496]{1,0:T(8,128)(2,1)S(1)}, bf16[168,496]{1,0:T(8,128)(2,1)S(1)}, u32[]{:S(2)}, u32[]{:S(2)}) collective-permute-start(bf16[168,496]{1,0:T(8,128)(2,1)S(1)} %fusion.66), channel_id=1, source_target_pairs={{0,2},{2,0},{1,3},{3,1},{4,6},{6,4},{5,7},{7,5},{8,10},{10,8},{9,1... | collective-permute-start | bytes 499976 | tf_op jit(solution)/shard_map/ppermute | solution.py:20
  48.6 3.0 %collective-permute-done.13 = bf16[168,512]{1,0:T(8,128)(2,1)S(1)} collective-permute-done((bf16[168,512]{1,0:T(8,128)(2,1)S(1)}, bf16[168,512]{1,0:T(8,128)(2,1)S(1)}, u32[]{:S(2)}, u32[]{:S(2)}) %collective-permute-start.13) | collective-permute-done | bytes 172064 | tf_op jit(solution)/shard_map/ppermute | solution.py:20
  51.7 5.4 %collective-permute-start.14 = (bf16[168,512]{1,0:T(8,128)(2,1)S(1)}, bf16[168,512]{1,0:T(8,128)(2,1)S(1)}, u32[]{:S(2)}, u32[]{:S(2)}) collective-permute-start(bf16[168,512]{1,0:T(8,128)(2,1)S(1)} %fusion.65), channel_id=1, source_target_pairs={{0,2},{2,0},{1,3},{3,1},{4,6},{6,4},{5,7},{7,5},{8,10},{10,8},{9,1... | collective-permute-start | bytes 516104 | tf_op jit(solution)/shard_map/ppermute | solution.py:20
  60.6 3.7 %collective-permute-done.14 = bf16[168,512]{1,0:T(8,128)(2,1)S(1)} collective-permute-done((bf16[168,512]{1,0:T(8,128)(2,1)S(1)}, bf16[168,512]{1,0:T(8,128)(2,1)S(1)}, u32[]{:S(2)}, u32[]{:S(2)}) %collective-permute-start.14) | collective-permute-done | bytes 172064 | tf_op jit(solution)/shard_map/ppermute | solution.py:20
  65.1 2.9 %collective-permute-start.17 = (bf16[168,512]{1,0:T(8,128)(2,1)S(1)}, bf16[168,512]{1,0:T(8,128)(2,1)S(1)}, u32[]{:S(2)}, u32[]{:S(2)}) collective-permute-start(bf16[168,512]{1,0:T(8,128)(2,1)S(1)} %get-tuple-element.10), channel_id=1, source_target_pairs={{0,12},{4,8},{8,4},{12,0},{1,13},{5,9},{9,5},{13,1},{2,14},{6,10},... | collective-permute-start | bytes 516104 | tf_op jit(solution)/shard_map/ppermute | solution.py:20
  68.0 5.0 %collective-permute-done.15 = bf16[168,512]{1,0:T(8,128)(2,1)S(1)} collective-permute-done((bf16[168,512]{1,0:T(8,128)(2,1)S(1)}, bf16[168,512]{1,0:T(8,128)(2,1)S(1)}, u32[]{:S(2)}, u32[]{:S(2)}) %collective-permute-start.15) | collective-permute-done | bytes 172064 | tf_op jit(solution)/shard_map/ppermute | solution.py:20
  73.1 4.7 %collective-permute-start.18 = (bf16[4,168,512]{2,1,0:T(8,128)(2,1)S(1)}, bf16[4,168,512]{2,1,0:T(8,128)(2,1)S(1)}, u32[]{:S(2)}, u32[]{:S(2)}) collective-permute-start(bf16[4,168,512]{2,1,0:T(8,128)(2,1)S(1)} %bitcast_dynamic-update-slice_fusion.8), channel_id=1, source_target_pairs={{0,1},{1,0},{2,3},{3,2},{4,5},{5,4},{6,7},{7,6},{8,9},{9,8},{10,11... | collective-permute-start | bytes 2064392 | tf_op jit(solution)/shard_map/ppermute | solution.py:20
  82.7 5.1 %collective-permute-start.28 = (bf16[336,640]{1,0:T(8,128)(2,1)S(1)}, bf16[336,640]{1,0:T(8,128)(2,1)S(1)}, u32[]{:S(2)}, u32[]{:S(2)}) collective-permute-start(bf16[336,640]{1,0:T(8,128)(2,1)S(1)} %get-tuple-element.20), channel_id=1, source_target_pairs={{0,48},{32,16},{1,49},{33,17},{2,50},{34,18},{3,51},{35,19},{4,52}... | collective-permute-start | bytes 1290248 | tf_op jit(solution)/shard_map/ppermute | solution.py:65
  87.8 2.3 %fusion.79 = (bf16[1344,640]{1,0:T(8,128)(2,1)S(1)}, f32[1344,640]{1,0:T(8,128)S(1)}) fusion(bf16[1344,1008]{1,0:T(8,128)(2,1)S(1)} %bitcast.62, bf16[336,640]{1,0:T(8,128)(2,1)S(1)} %copy-done, bf16[336,640]{1,0:T(8,128)(2,1)S(1)} %collective-permute-done.9, bf16[336,640]{1,0:T(8,128)(2,1)S(1)} %collective-permute-done.7), kind=kOutput, calls=%fused_computation.107 | convolution fusion | flops 1738813440 | bytes 9160704 | tf_op jit(solution)/shard_map/dot_general | solution.py:36
  94.7 6.2 %collective-permute-done.28 = bf16[336,640]{1,0:T(8,128)(2,1)S(1)} collective-permute-done((bf16[336,640]{1,0:T(8,128)(2,1)S(1)}, bf16[336,640]{1,0:T(8,128)(2,1)S(1)}, u32[]{:S(2)}, u32[]{:S(2)}) %collective-permute-start.28) | collective-permute-done | bytes 430112 | tf_op jit(solution)/shard_map/ppermute | solution.py:65
  102.0 10.1 %collective-permute-done.30 = bf16[336,640]{1,0:T(8,128)(2,1)S(1)} collective-permute-done((bf16[336,640]{1,0:T(8,128)(2,1)S(1)}, bf16[336,640]{1,0:T(8,128)(2,1)S(1)}, u32[]{:S(2)}, u32[]{:S(2)}) %collective-permute-start.30) | collective-permute-done | bytes 430112 | tf_op jit(solution)/shard_map/ppermute | solution.py:24
  117.9 5.7 %collective-permute-done.36 = bf16[336,640]{1,0:T(8,128)(2,1)S(1)} collective-permute-done((bf16[336,640]{1,0:T(8,128)(2,1)S(1)}, bf16[336,640]{1,0:T(8,128)(2,1)S(1)}, u32[]{:S(2)}, u32[]{:S(2)}) %collective-permute-start.36) | collective-permute-done | bytes 430112 | tf_op jit(solution)/shard_map/ppermute | solution.py:24
  123.6 8.5 %collective-permute-done.35 = bf16[336,640]{1,0:T(8,128)(2,1)S(1)} collective-permute-done((bf16[336,640]{1,0:T(8,128)(2,1)S(1)}, bf16[336,640]{1,0:T(8,128)(2,1)S(1)}, u32[]{:S(2)}, u32[]{:S(2)}) %collective-permute-start.35) | collective-permute-done | bytes 430112 | tf_op jit(solution)/shard_map/ppermute | solution.py:24
  132.1 2.2 %collective-permute-done.34 = bf16[336,640]{1,0:T(8,128)(2,1)S(1)} collective-permute-done((bf16[336,640]{1,0:T(8,128)(2,1)S(1)}, bf16[336,640]{1,0:T(8,128)(2,1)S(1)}, u32[]{:S(2)}, u32[]{:S(2)}) %collective-permute-start.34) | collective-permute-done | bytes 430112 | tf_op jit(solution)/shard_map/ppermute | solution.py:24
  136.3 3.9 %collective-permute-start.38 = (bf16[336,640]{1,0:T(8,128)(2,1)S(1)}, bf16[336,640]{1,0:T(8,128)(2,1)S(1)}, u32[]{:S(2)}, u32[]{:S(2)}) collective-permute-start(bf16[336,640]{1,0:T(8,128)(2,1)S(1)} %get-tuple-element.18), channel_id=1, source_target_pairs={{0,48},{32,16},{1,49},{33,17},{2,50},{34,18},{3,51},{35,19},{4,52}... | collective-permute-start | bytes 1290248 | tf_op jit(solution)/shard_map/ppermute | solution.py:65
  140.2 2.3 %fusion.80 = (bf16[1344,640]{1,0:T(8,128)(2,1)S(1)}, f32[1344,640]{1,0:T(8,128)S(1)}) fusion(bf16[1344,1008]{1,0:T(8,128)(2,1)S(1)} %bitcast.64, bf16[336,640]{1,0:T(8,128)(2,1)S(1)} %get-tuple-element.5, bf16[336,640]{1,0:T(8,128)(2,1)S(1)} %collective-permute-done.33, bf16[336,640]{1,0:T(8,128)(2,1)S(1)} %collective-permute-done.32), kind=kOutput, calls=%fused_computation.108 | convolution fusion | flops 1738813440 | bytes 9160704 | tf_op jit(solution)/shard_map/dot_general | solution.py:36
  148.3 5.1 %collective-permute-done.38 = bf16[336,640]{1,0:T(8,128)(2,1)S(1)} collective-permute-done((bf16[336,640]{1,0:T(8,128)(2,1)S(1)}, bf16[336,640]{1,0:T(8,128)(2,1)S(1)}, u32[]{:S(2)}, u32[]{:S(2)}) %collective-permute-start.38) | collective-permute-done | bytes 430112 | tf_op jit(solution)/shard_map/ppermute | solution.py:65
  154.7 10.7 %collective-permute-done.40 = bf16[336,640]{1,0:T(8,128)(2,1)S(1)} collective-permute-done((bf16[336,640]{1,0:T(8,128)(2,1)S(1)}, bf16[336,640]{1,0:T(8,128)(2,1)S(1)}, u32[]{:S(2)}, u32[]{:S(2)}) %collective-permute-start.40) | collective-permute-done | bytes 430112 | tf_op jit(solution)/shard_map/ppermute | solution.py:24
  (102 shorter events, 52.1 us)
Async XLA Ops:
  2.1 23.0 %collective-permute-start.9 = (bf16[336,640]{1,0:T(8,128)(2,1)}, bf16[336,640]{1,0:T(8,128)(2,1)S(1)}, u32[]{:S(2)}, u32[]{:S(2)}) collective-permute-start(bf16[336,640]{1,0:T(8,128)(2,1)} %param.1), channel_id=1, source_target_pairs={{48,0},{16,32},{49,1},{17,33},{50,2},{18,34},{51,3},{19,35},{52,4}... | collective-permute-start | bytes 1290248 | tf_op jit(solution)/shard_map/ppermute | solution.py:52
  3.4 25.5 %collective-permute-start.7 = (bf16[336,640]{1,0:T(8,128)(2,1)}, bf16[336,640]{1,0:T(8,128)(2,1)S(1)}, u32[]{:S(2)}, u32[]{:S(2)}) collective-permute-start(bf16[336,640]{1,0:T(8,128)(2,1)} %param.1), channel_id=1, source_target_pairs={{16,0},{48,16},{0,32},{32,48},{17,1},{49,17},{1,33},{33,49},{18,2}... | collective-permute-start | bytes 1290248 | tf_op jit(solution)/shard_map/ppermute | solution.py:52
  6.5 17.0 %collective-permute-start.3 = (bf16[336,640]{1,0:T(8,128)(2,1)}, bf16[336,640]{1,0:T(8,128)(2,1)S(1)}, u32[]{:S(2)}, u32[]{:S(2)}) collective-permute-start(bf16[336,640]{1,0:T(8,128)(2,1)} %param.1), channel_id=1, source_target_pairs={{0,128},{64,192},{128,0},{192,64},{1,129},{65,193},{129,1},{193,65... | collective-permute-start | bytes 1290248 | tf_op jit(solution)/shard_map/ppermute | solution.py:24
  9.1 18.3 %collective-permute-start.1 = (bf16[336,640]{1,0:T(8,128)(2,1)}, bf16[336,640]{1,0:T(8,128)(2,1)S(1)}, u32[]{:S(2)}, u32[]{:S(2)}) collective-permute-start(bf16[336,640]{1,0:T(8,128)(2,1)} %param.1), channel_id=1, source_target_pairs={{0,192},{64,0},{128,64},{192,128},{1,193},{65,1},{129,65},{193,129... | collective-permute-start | bytes 1290248 | tf_op jit(solution)/shard_map/ppermute | solution.py:24
  11.4 17.6 %collective-permute-start = (bf16[336,640]{1,0:T(8,128)(2,1)}, bf16[336,640]{1,0:T(8,128)(2,1)S(1)}, u32[]{:S(2)}, u32[]{:S(2)}) collective-permute-start(bf16[336,640]{1,0:T(8,128)(2,1)} %param.1), channel_id=1, source_target_pairs={{0,1},{1,0},{2,3},{3,2},{4,5},{5,4},{6,7},{7,6},{8,9},{9,8},{10,11... | collective-permute-start | bytes 1290248 | tf_op jit(solution)/shard_map/ppermute | solution.py:20
  36.6 12.0 %collective-permute-start.11 = (bf16[168,512]{1,0:T(8,128)(2,1)S(1)}, bf16[168,512]{1,0:T(8,128)(2,1)S(1)}, u32[]{:S(2)}, u32[]{:S(2)}) collective-permute-start(bf16[168,512]{1,0:T(8,128)(2,1)S(1)} %get-tuple-element.24), channel_id=1, source_target_pairs={{0,4},{4,0},{8,12},{12,8},{1,5},{5,1},{9,13},{13,9},{2,6},{6,2},{1... | collective-permute-start | bytes 516104 | tf_op jit(solution)/shard_map/ppermute | solution.py:20
  37.5 14.1 %collective-permute-start.13 = (bf16[168,512]{1,0:T(8,128)(2,1)S(1)}, bf16[168,512]{1,0:T(8,128)(2,1)S(1)}, u32[]{:S(2)}, u32[]{:S(2)}) collective-permute-start(bf16[168,512]{1,0:T(8,128)(2,1)S(1)} %get-tuple-element.25), channel_id=1, source_target_pairs={{0,12},{4,8},{8,4},{12,0},{1,13},{5,9},{9,5},{13,1},{2,14},{6,10},... | collective-permute-start | bytes 516104 | tf_op jit(solution)/shard_map/ppermute | solution.py:20
  39.3 12.3 %collective-permute-start.12 = (bf16[168,512]{1,0:T(8,128)(2,1)S(1)}, bf16[168,512]{1,0:T(8,128)(2,1)S(1)}, u32[]{:S(2)}, u32[]{:S(2)}) collective-permute-start(bf16[168,512]{1,0:T(8,128)(2,1)S(1)} %get-tuple-element.26), channel_id=1, source_target_pairs={{0,8},{4,12},{8,0},{12,4},{1,9},{5,13},{9,1},{13,5},{2,10},{6,14},... | collective-permute-start | bytes 516104 | tf_op jit(solution)/shard_map/ppermute | solution.py:20
  43.4 13.7 %collective-permute-start.22 = (bf16[168,496]{1,0:T(8,128)(2,1)S(1)}, bf16[168,496]{1,0:T(8,128)(2,1)S(1)}, u32[]{:S(2)}, u32[]{:S(2)}) collective-permute-start(bf16[168,496]{1,0:T(8,128)(2,1)S(1)} %fusion.66), channel_id=1, source_target_pairs={{0,2},{2,0},{1,3},{3,1},{4,6},{6,4},{5,7},{7,5},{8,10},{10,8},{9,1... | collective-permute-start | bytes 499976 | tf_op jit(solution)/shard_map/ppermute | solution.py:20
  51.7 12.6 %collective-permute-start.14 = (bf16[168,512]{1,0:T(8,128)(2,1)S(1)}, bf16[168,512]{1,0:T(8,128)(2,1)S(1)}, u32[]{:S(2)}, u32[]{:S(2)}) collective-permute-start(bf16[168,512]{1,0:T(8,128)(2,1)S(1)} %fusion.65), channel_id=1, source_target_pairs={{0,2},{2,0},{1,3},{3,1},{4,6},{6,4},{5,7},{7,5},{8,10},{10,8},{9,1... | collective-permute-start | bytes 516104 | tf_op jit(solution)/shard_map/ppermute | solution.py:20
  57.3 20.6 %collective-permute-start.24 = (bf16[168,496]{1,0:T(8,128)(2,1)S(1)}, bf16[168,496]{1,0:T(8,128)(2,1)S(1)}, u32[]{:S(2)}, u32[]{:S(2)}) collective-permute-start(bf16[168,496]{1,0:T(8,128)(2,1)S(1)} %get-tuple-element.8), channel_id=1, source_target_pairs={{0,8},{4,12},{8,0},{12,4},{1,9},{5,13},{9,1},{13,5},{2,10},{6,14},... | collective-permute-start | bytes 499976 | tf_op jit(solution)/shard_map/ppermute | solution.py:20
  58.7 19.2 %collective-permute-start.25 = (bf16[168,496]{1,0:T(8,128)(2,1)S(1)}, bf16[168,496]{1,0:T(8,128)(2,1)S(1)}, u32[]{:S(2)}, u32[]{:S(2)}) collective-permute-start(bf16[168,496]{1,0:T(8,128)(2,1)S(1)} %get-tuple-element.8), channel_id=1, source_target_pairs={{0,12},{4,8},{8,4},{12,0},{1,13},{5,9},{9,5},{13,1},{2,14},{6,10},... | collective-permute-start | bytes 499976 | tf_op jit(solution)/shard_map/ppermute | solution.py:20
  82.6 12.1 %collective-permute-start.27 = (bf16[336,640]{1,0:T(8,128)(2,1)S(1)}, bf16[336,640]{1,0:T(8,128)(2,1)S(1)}, u32[]{:S(2)}, u32[]{:S(2)}) collective-permute-start(bf16[336,640]{1,0:T(8,128)(2,1)S(1)} %get-tuple-element.19), channel_id=1, source_target_pairs={{0,16},{16,48},{32,0},{48,32},{1,17},{17,49},{33,1},{49,33},{2,18}... | collective-permute-start | bytes 1290248 | tf_op jit(solution)/shard_map/ppermute | solution.py:64
  82.7 18.2 %collective-permute-start.28 = (bf16[336,640]{1,0:T(8,128)(2,1)S(1)}, bf16[336,640]{1,0:T(8,128)(2,1)S(1)}, u32[]{:S(2)}, u32[]{:S(2)}) collective-permute-start(bf16[336,640]{1,0:T(8,128)(2,1)S(1)} %get-tuple-element.20), channel_id=1, source_target_pairs={{0,48},{32,16},{1,49},{33,17},{2,50},{34,18},{3,51},{35,19},{4,52}... | collective-permute-start | bytes 1290248 | tf_op jit(solution)/shard_map/ppermute | solution.py:65
  90.2 11.8 %collective-permute-start.29 = (bf16[336,640]{1,0:T(8,128)(2,1)S(1)}, bf16[336,640]{1,0:T(8,128)(2,1)S(1)}, u32[]{:S(2)}, u32[]{:S(2)}) collective-permute-start(bf16[336,640]{1,0:T(8,128)(2,1)S(1)} %get-tuple-element.14), channel_id=1, source_target_pairs={{0,64},{64,128},{128,192},{192,0},{1,65},{65,129},{129,193},{193,1... | collective-permute-start | bytes 1290248 | tf_op jit(solution)/shard_map/ppermute | solution.py:24
  93.0 19.1 %collective-permute-start.30 = (bf16[336,640]{1,0:T(8,128)(2,1)S(1)}, bf16[336,640]{1,0:T(8,128)(2,1)S(1)}, u32[]{:S(2)}, u32[]{:S(2)}) collective-permute-start(bf16[336,640]{1,0:T(8,128)(2,1)S(1)} %get-tuple-element.16), channel_id=1, source_target_pairs={{0,128},{64,192},{128,0},{192,64},{1,129},{65,193},{129,1},{193,65... | collective-permute-start | bytes 1290248 | tf_op jit(solution)/shard_map/ppermute | solution.py:24
  113.1 19.1 %collective-permute-start.35 = (bf16[336,640]{1,0:T(8,128)(2,1)S(1)}, bf16[336,640]{1,0:T(8,128)(2,1)S(1)}, u32[]{:S(2)}, u32[]{:S(2)}) collective-permute-start(bf16[336,640]{1,0:T(8,128)(2,1)S(1)} %get-tuple-element.5), channel_id=1, source_target_pairs={{0,128},{64,192},{128,0},{192,64},{1,129},{65,193},{129,1},{193,65... | collective-permute-start | bytes 1290248 | tf_op jit(solution)/shard_map/ppermute | solution.py:24
  115.2 19.1 %collective-permute-start.34 = (bf16[336,640]{1,0:T(8,128)(2,1)S(1)}, bf16[336,640]{1,0:T(8,128)(2,1)S(1)}, u32[]{:S(2)}, u32[]{:S(2)}) collective-permute-start(bf16[336,640]{1,0:T(8,128)(2,1)S(1)} %get-tuple-element.5), channel_id=1, source_target_pairs={{0,192},{64,0},{128,64},{192,128},{1,193},{65,1},{129,65},{193,129... | collective-permute-start | bytes 1290248 | tf_op jit(solution)/shard_map/ppermute | solution.py:24
  115.6 24.6 %collective-permute-start.33 = (bf16[336,640]{1,0:T(8,128)(2,1)S(1)}, bf16[336,640]{1,0:T(8,128)(2,1)S(1)}, u32[]{:S(2)}, u32[]{:S(2)}) collective-permute-start(bf16[336,640]{1,0:T(8,128)(2,1)S(1)} %get-tuple-element.5), channel_id=1, source_target_pairs={{48,0},{16,32},{49,1},{17,33},{50,2},{18,34},{51,3},{19,35},{52,4}... | collective-permute-start | bytes 1290248 | tf_op jit(solution)/shard_map/ppermute | solution.py:52
  116.8 23.4 %collective-permute-start.32 = (bf16[336,640]{1,0:T(8,128)(2,1)S(1)}, bf16[336,640]{1,0:T(8,128)(2,1)S(1)}, u32[]{:S(2)}, u32[]{:S(2)}) collective-permute-start(bf16[336,640]{1,0:T(8,128)(2,1)S(1)} %get-tuple-element.5), channel_id=1, source_target_pairs={{16,0},{48,16},{0,32},{32,48},{17,1},{49,17},{1,33},{33,49},{18,2}... | collective-permute-start | bytes 1290248 | tf_op jit(solution)/shard_map/ppermute | solution.py:52
  136.2 12.1 %collective-permute-start.37 = (bf16[336,640]{1,0:T(8,128)(2,1)S(1)}, bf16[336,640]{1,0:T(8,128)(2,1)S(1)}, u32[]{:S(2)}, u32[]{:S(2)}) collective-permute-start(bf16[336,640]{1,0:T(8,128)(2,1)S(1)} %get-tuple-element.17), channel_id=1, source_target_pairs={{0,16},{16,48},{32,0},{48,32},{1,17},{17,49},{33,1},{49,33},{2,18}... | collective-permute-start | bytes 1290248 | tf_op jit(solution)/shard_map/ppermute | solution.py:64
  136.3 17.1 %collective-permute-start.38 = (bf16[336,640]{1,0:T(8,128)(2,1)S(1)}, bf16[336,640]{1,0:T(8,128)(2,1)S(1)}, u32[]{:S(2)}, u32[]{:S(2)}) collective-permute-start(bf16[336,640]{1,0:T(8,128)(2,1)S(1)} %get-tuple-element.18), channel_id=1, source_target_pairs={{0,48},{32,16},{1,49},{33,17},{2,50},{34,18},{3,51},{35,19},{4,52}... | collective-permute-start | bytes 1290248 | tf_op jit(solution)/shard_map/ppermute | solution.py:65
  142.7 12.0 %collective-permute-start.39 = (bf16[336,640]{1,0:T(8,128)(2,1)S(1)}, bf16[336,640]{1,0:T(8,128)(2,1)S(1)}, u32[]{:S(2)}, u32[]{:S(2)}) collective-permute-start(bf16[336,640]{1,0:T(8,128)(2,1)S(1)} %get-tuple-element.11), channel_id=1, source_target_pairs={{0,64},{64,128},{128,192},{192,0},{1,65},{65,129},{129,193},{193,1... | collective-permute-start | bytes 1290248 | tf_op jit(solution)/shard_map/ppermute | solution.py:24
  146.3 19.2 %collective-permute-start.40 = (bf16[336,640]{1,0:T(8,128)(2,1)S(1)}, bf16[336,640]{1,0:T(8,128)(2,1)S(1)}, u32[]{:S(2)}, u32[]{:S(2)}) collective-permute-start(bf16[336,640]{1,0:T(8,128)(2,1)S(1)} %get-tuple-element.13), channel_id=1, source_target_pairs={{0,128},{64,192},{128,0},{192,64},{1,129},{65,193},{129,1},{193,65... | collective-permute-start | bytes 1290248 | tf_op jit(solution)/shard_map/ppermute | solution.py:24
  (19 other events, 137.2 us)
where the time goes:
time: 167 us
  waiting for transfers between devices  80.7 us (48%)
  starting transfers between devices  70.3 us (42%)
  matrix products  10.5 us (6%)
  other arithmetic  3.32 us (2%)
    ppermute x12, waiting for transfers between devices, send_up(): return lax.ppermute(v, axis, [(i, (i + k) % size) for i in range(size)])  50.7 us
    ppermute x22, starting transfers between devices, send_xor(): return lax.ppermute(v, axis, [(i, i ^ k) for i in range(size)])  36.4 us
    ppermute x12, starting transfers between devices, send_up(): return lax.ppermute(v, axis, [(i, (i + k) % size) for i in range(size)])  18 us
    ppermute x22, waiting for transfers between devices, send_xor(): return lax.ppermute(v, axis, [(i, i ^ k) for i in range(size)])  17.7 us
    ppermute x2, waiting for transfers between devices, apply_gram(): lax.ppermute(back[B:], 'zl', [(b, a) for a, b in SLOT_B])  11.3 us
    dot_general x6, matrix products, dot(): lax.dot_general(a, b, (((da,), (db,)), ((), ())), preferred_element_type=...  10.5 us
    ppermute x2, starting transfers between devices, apply_gram(): lax.ppermute(back[B:], 'zl', [(b, a) for a, b in SLOT_B])  8.96 us
    ppermute x4, starting transfers between devices, fetch_z(): return [lax.ppermute(v, 'zl', SLOT_A), lax.ppermute(v, 'zl', SLOT_B)]  6.71 us
  transfers between devices with their start and end apart: 42, of which 22 were waited for; matrix products, arithmetic and copies ran while one was open for 7% of the time, Pallas kernels for 0%

commit v1 on v0

--- a/solution.py
+++ b/solution.py
@@ -59,12 +59,12 @@
 def apply_gram(gram, columns, rows):
     part = dot(gram, columns, 1, 0)
     back = narrow(dot(gram[:, : 2 * B], rows, 0, 0))
-    sent = narrow(part)
+    sent, back = lax.optimization_barrier((narrow(part), back))
     total = part[:B]
+    for s in OFFSETS:
+        total = total + wide(send_up(sent[s * B : (s + 1) * B], "y", 4, s))
     total = total + wide(lax.ppermute(back[:B], "zl", [(b, a) for a, b in SLOT_A]))
     total = total + wide(lax.ppermute(back[B:], "zl", [(b, a) for a, b in SLOT_B]))
-    for s in OFFSETS:
-        total = total + wide(send_up(sent[s * B : (s + 1) * B], "y", 4, s))
     return total
 
 
@@ -89,8 +89,8 @@
 def body(momentum):
     core = lax.axis_index("core")
     xi = lax.axis_index("x")
+    y = fetch_y(momentum)
     za, zb = fetch_z(momentum)
-    y = fetch_y(momentum)
     m_o = swap(momentum)
     rows = [jnp.concatenate([pick(core, momentum), pick(core, m_o)], axis=1)]
     rows += [jnp.concatenate([pick(core, v), swap(pick(1 - core, v))], axis=1) for v in y]
@@ -116,8 +116,9 @@
     columns = jnp.concatenate([za, zb, momentum], axis=0)
     first = apply_gram(gram, columns, jnp.concatenate([momentum] + y, axis=0))
     sent = narrow(first)
+    rows = jnp.concatenate([sent] + fetch_y(sent), axis=0)
     columns = jnp.concatenate(fetch_z(sent) + [sent], axis=0)
-    second = apply_gram(gram, columns, jnp.concatenate([sent] + fetch_y(sent), axis=0))
+    second = apply_gram(gram, columns, rows)
     return narrow(coef_a * wide(momentum) + coef_b * first + coef_c * second)
 
 

time: 167 us -> 162 us (0.970); the launches traced: 167 us -> 160 us
  waiting for transfers between devices: 80.7 us -> 69.3 us
  starting transfers between devices: 70.3 us -> 74.6 us
    ppermute x4, waiting for transfers between devices: 0.01 us -> 14.8 us  [fetch_z(): return [lax.ppermute(v, 'zl', SLOT_A), lax.ppermute(v, 'zl', SLOT_B)]]
    ppermute x12, waiting for transfers between devices: 50.7 us -> 36.8 us  [send_up(): return lax.ppermute(v, axis, [(i, (i + k) % size) for i in range(size)])]
    ppermute x2, waiting for transfers between devices: 11.3 us -> 0.01 us  [apply_gram(): lax.ppermute(back[B:], 'zl', [(b, a) for a, b in SLOT_B])]
    ppermute x2, starting transfers between devices: 8.96 us -> 10.9 us  [apply_gram(): lax.ppermute(back[B:], 'zl', [(b, a) for a, b in SLOT_B])]
  transfers between devices with their start and end apart: 42 -> 42, of which waited for: 22 -> 19; matrix products, arithmetic and copies ran while one was open for 7% -> 5% of each run, Pallas kernels for 0% -> 0%
where the time goes in v1:
time: 162 us; the launch traced here: 160 us
  starting transfers between devices  74.6 us (46%)
  waiting for transfers between devices  69.3 us (43%)
  matrix products  10.5 us (6%)
  other arithmetic  3.32 us (2%)
    ppermute x12, waiting for transfers between devices, send_up(): return lax.ppermute(v, axis, [(i, (i + k) % size) for i in range(size)])  36.8 us
    ppermute x22, starting transfers between devices, send_xor(): return lax.ppermute(v, axis, [(i, i ^ k) for i in range(size)])  36.4 us
    ppermute x12, starting transfers between devices, send_up(): return lax.ppermute(v, axis, [(i, (i + k) % size) for i in range(size)])  18.1 us
    ppermute x22, waiting for transfers between devices, send_xor(): return lax.ppermute(v, axis, [(i, i ^ k) for i in range(size)])  17.7 us
    ppermute x4, waiting for transfers between devices, fetch_z(): return [lax.ppermute(v, 'zl', SLOT_A), lax.ppermute(v, 'zl', SLOT_B)]  14.8 us
    ppermute x2, starting transfers between devices, apply_gram(): lax.ppermute(back[B:], 'zl', [(b, a) for a, b in SLOT_B])  10.9 us
    dot_general x6, matrix products, dot(): lax.dot_general(a, b, (((da,), (db,)), ((), ())), preferred_element_type=...  10.5 us
    ppermute x4, starting transfers between devices, fetch_z(): return [lax.ppermute(v, 'zl', SLOT_A), lax.ppermute(v, 'zl', SLOT_B)]  7.68 us
  transfers between devices with their start and end apart: 42, of which 19 were waited for; matrix products, arithmetic and copies ran while one was open for 5% of the time, Pallas kernels for 0%

profile of v1, /device:TPU:1, one launch (start us, length us, event | category | flops | bytes accessed | tf_op | source)
XLA Modules:
  0.0 159.6 jit_solution(9977786510580627606)
XLA Ops:
  0.0 2.1 %collective-permute-start.5 = (bf16[336,640]{1,0:T(8,128)(2,1)}, bf16[336,640]{1,0:T(8,128)(2,1)S(1)}, u32[]{:S(2)}, u32[]{:S(2)}) collective-permute-start(bf16[336,640]{1,0:T(8,128)(2,1)} %param.1), channel_id=1, source_target_pairs={{0,64},{64,128},{128,192},{192,0},{1,65},{65,129},{129,193},{193,1... | collective-permute-start | bytes 1290248 | tf_op jit(solution)/shard_map/ppermute | solution.py:24
  3.4 3.1 %collective-permute-start.7 = (bf16[336,640]{1,0:T(8,128)(2,1)}, bf16[336,640]{1,0:T(8,128)(2,1)S(1)}, u32[]{:S(2)}, u32[]{:S(2)}) collective-permute-start(bf16[336,640]{1,0:T(8,128)(2,1)} %param.1), channel_id=1, source_target_pairs={{16,0},{48,16},{0,32},{32,48},{17,1},{49,17},{1,33},{33,49},{18,2}... | collective-permute-start | bytes 1290248 | tf_op jit(solution)/shard_map/ppermute | solution.py:52
  6.5 2.6 %collective-permute-start.3 = (bf16[336,640]{1,0:T(8,128)(2,1)}, bf16[336,640]{1,0:T(8,128)(2,1)S(1)}, u32[]{:S(2)}, u32[]{:S(2)}) collective-permute-start(bf16[336,640]{1,0:T(8,128)(2,1)} %param.1), channel_id=1, source_target_pairs={{0,128},{64,192},{128,0},{192,64},{1,129},{65,193},{129,1},{193,65... | collective-permute-start | bytes 1290248 | tf_op jit(solution)/shard_map/ppermute | solution.py:24
  11.4 3.3 %collective-permute-start = (bf16[336,640]{1,0:T(8,128)(2,1)}, bf16[336,640]{1,0:T(8,128)(2,1)S(1)}, u32[]{:S(2)}, u32[]{:S(2)}) collective-permute-start(bf16[336,640]{1,0:T(8,128)(2,1)} %param.1), channel_id=1, source_target_pairs={{0,1},{1,0},{2,3},{3,2},{4,5},{5,4},{6,7},{7,6},{8,9},{9,8},{10,11... | collective-permute-start | bytes 1290248 | tf_op jit(solution)/shard_map/ppermute | solution.py:20
  14.7 8.8 %collective-permute-done.3 = bf16[336,640]{1,0:T(8,128)(2,1)S(1)} collective-permute-done((bf16[336,640]{1,0:T(8,128)(2,1)}, bf16[336,640]{1,0:T(8,128)(2,1)S(1)}, u32[]{:S(2)}, u32[]{:S(2)}) %collective-permute-start.3) | collective-permute-done | bytes 430112 | tf_op jit(solution)/shard_map/ppermute | solution.py:24
  25.2 2.2 %collective-permute-done.1 = bf16[336,640]{1,0:T(8,128)(2,1)S(1)} collective-permute-done((bf16[336,640]{1,0:T(8,128)(2,1)}, bf16[336,640]{1,0:T(8,128)(2,1)S(1)}, u32[]{:S(2)}, u32[]{:S(2)}) %collective-permute-start.1) | collective-permute-done | bytes 430112 | tf_op jit(solution)/shard_map/ppermute | solution.py:24
  40.9 2.4 %collective-permute-done.20 = bf16[168,496]{1,0:T(8,128)(2,1)S(1)} collective-permute-done((bf16[168,496]{1,0:T(8,128)(2,1)S(1)}, bf16[168,496]{1,0:T(8,128)(2,1)S(1)}, u32[]{:S(2)}, u32[]{:S(2)}) %collective-permute-start.20) | collective-permute-done | bytes 166688 | tf_op jit(solution)/shard_map/ppermute | solution.py:20
  43.4 5.2 %collective-permute-start.22 = (bf16[168,496]{1,0:T(8,128)(2,1)S(1)}, bf16[168,496]{1,0:T(8,128)(2,1)S(1)}, u32[]{:S(2)}, u32[]{:S(2)}) collective-permute-start(bf16[168,496]{1,0:T(8,128)(2,1)S(1)} %fusion.66), channel_id=1, source_target_pairs={{0,2},{2,0},{1,3},{3,1},{4,6},{6,4},{5,7},{7,5},{8,10},{10,8},{9,1... | collective-permute-start | bytes 499976 | tf_op jit(solution)/shard_map/ppermute | solution.py:20
  48.6 3.0 %collective-permute-done.13 = bf16[168,512]{1,0:T(8,128)(2,1)S(1)} collective-permute-done((bf16[168,512]{1,0:T(8,128)(2,1)S(1)}, bf16[168,512]{1,0:T(8,128)(2,1)S(1)}, u32[]{:S(2)}, u32[]{:S(2)}) %collective-permute-start.13) | collective-permute-done | bytes 172064 | tf_op jit(solution)/shard_map/ppermute | solution.py:20
  51.7 5.4 %collective-permute-start.14 = (bf16[168,512]{1,0:T(8,128)(2,1)S(1)}, bf16[168,512]{1,0:T(8,128)(2,1)S(1)}, u32[]{:S(2)}, u32[]{:S(2)}) collective-permute-start(bf16[168,512]{1,0:T(8,128)(2,1)S(1)} %fusion.65), channel_id=1, source_target_pairs={{0,2},{2,0},{1,3},{3,1},{4,6},{6,4},{5,7},{7,5},{8,10},{10,8},{9,1... | collective-permute-start | bytes 516104 | tf_op jit(solution)/shard_map/ppermute | solution.py:20
  60.6 3.7 %collective-permute-done.14 = bf16[168,512]{1,0:T(8,128)(2,1)S(1)} collective-permute-done((bf16[168,512]{1,0:T(8,128)(2,1)S(1)}, bf16[168,512]{1,0:T(8,128)(2,1)S(1)}, u32[]{:S(2)}, u32[]{:S(2)}) %collective-permute-start.14) | collective-permute-done | bytes 172064 | tf_op jit(solution)/shard_map/ppermute | solution.py:20
  65.1 2.9 %collective-permute-start.17 = (bf16[168,512]{1,0:T(8,128)(2,1)S(1)}, bf16[168,512]{1,0:T(8,128)(2,1)S(1)}, u32[]{:S(2)}, u32[]{:S(2)}) collective-permute-start(bf16[168,512]{1,0:T(8,128)(2,1)S(1)} %get-tuple-element.18), channel_id=1, source_target_pairs={{0,12},{4,8},{8,4},{12,0},{1,13},{5,9},{9,5},{13,1},{2,14},{6,10},... | collective-permute-start | bytes 516104 | tf_op jit(solution)/shard_map/ppermute | solution.py:20
  68.0 5.0 %collective-permute-done.15 = bf16[168,512]{1,0:T(8,128)(2,1)S(1)} collective-permute-done((bf16[168,512]{1,0:T(8,128)(2,1)S(1)}, bf16[168,512]{1,0:T(8,128)(2,1)S(1)}, u32[]{:S(2)}, u32[]{:S(2)}) %collective-permute-start.15) | collective-permute-done | bytes 172064 | tf_op jit(solution)/shard_map/ppermute | solution.py:20
  73.1 4.7 %collective-permute-start.18 = (bf16[4,168,512]{2,1,0:T(8,128)(2,1)S(1)}, bf16[4,168,512]{2,1,0:T(8,128)(2,1)S(1)}, u32[]{:S(2)}, u32[]{:S(2)}) collective-permute-start(bf16[4,168,512]{2,1,0:T(8,128)(2,1)S(1)} %bitcast_dynamic-update-slice_fusion.8), channel_id=1, source_target_pairs={{0,1},{1,0},{2,3},{3,2},{4,5},{5,4},{6,7},{7,6},{8,9},{9,8},{10,11... | collective-permute-start | bytes 2064392 | tf_op jit(solution)/shard_map/ppermute | solution.py:20
  82.5 2.3 %fusion.79 = (bf16[1344,640]{1,0:T(8,128)(2,1)S(1)}, f32[1344,640]{1,0:T(8,128)S(1)}) fusion(bf16[1344,1008]{1,0:T(8,128)(2,1)S(1)} %bitcast.62, bf16[336,640]{1,0:T(8,128)(2,1)S(1)} %copy-done, bf16[336,640]{1,0:T(8,128)(2,1)S(1)} %collective-permute-done.9, bf16[336,640]{1,0:T(8,128)(2,1)S(1)} %collective-permute-done.7), kind=kOutput, calls=%fused_computation.107 | convolution fusion | flops 1738813440 | bytes 9160704 | tf_op jit(solution)/shard_map/dot_general | solution.py:36
  89.8 5.1 %collective-permute-start.31 = (bf16[336,640]{1,0:T(8,128)(2,1)S(1)}, bf16[336,640]{1,0:T(8,128)(2,1)S(1)}, u32[]{:S(2)}, u32[]{:S(2)}) collective-permute-start(bf16[336,640]{1,0:T(8,128)(2,1)S(1)} %get-tuple-element.28), channel_id=1, source_target_pairs={{0,48},{32,16},{1,49},{33,17},{2,50},{34,18},{3,51},{35,19},{4,52}... | collective-permute-start | bytes 1290248 | tf_op jit(solution)/shard_map/ppermute | solution.py:67
  94.9 2.5 %collective-permute-done.27 = bf16[336,640]{1,0:T(8,128)(2,1)S(1)} collective-permute-done((bf16[336,640]{1,0:T(8,128)(2,1)S(1)}, bf16[336,640]{1,0:T(8,128)(2,1)S(1)}, u32[]{:S(2)}, u32[]{:S(2)}) %collective-permute-start.27) | collective-permute-done | bytes 430112 | tf_op jit(solution)/shard_map/ppermute | solution.py:24
  97.4 10.1 %collective-permute-done.28 = bf16[336,640]{1,0:T(8,128)(2,1)S(1)} collective-permute-done((bf16[336,640]{1,0:T(8,128)(2,1)S(1)}, bf16[336,640]{1,0:T(8,128)(2,1)S(1)}, u32[]{:S(2)}, u32[]{:S(2)}) %collective-permute-start.28) | collective-permute-done | bytes 430112 | tf_op jit(solution)/shard_map/ppermute | solution.py:24
  111.7 2.1 %collective-permute-start.35 = (bf16[336,640]{1,0:T(8,128)(2,1)S(1)}, bf16[336,640]{1,0:T(8,128)(2,1)S(1)}, u32[]{:S(2)}, u32[]{:S(2)}) collective-permute-start(bf16[336,640]{1,0:T(8,128)(2,1)S(1)} %get-tuple-element.13), channel_id=1, source_target_pairs={{0,128},{64,192},{128,0},{192,64},{1,129},{65,193},{129,1},{193,65... | collective-permute-start | bytes 1290248 | tf_op jit(solution)/shard_map/ppermute | solution.py:24
  114.5 8.1 %collective-permute-done.33 = bf16[336,640]{1,0:T(8,128)(2,1)S(1)} collective-permute-done((bf16[336,640]{1,0:T(8,128)(2,1)S(1)}, bf16[336,640]{1,0:T(8,128)(2,1)S(1)}, u32[]{:S(2)}, u32[]{:S(2)}) %collective-permute-start.33) | collective-permute-done | bytes 430112 | tf_op jit(solution)/shard_map/ppermute | solution.py:52
  122.6 6.7 %collective-permute-done.32 = bf16[336,640]{1,0:T(8,128)(2,1)S(1)} collective-permute-done((bf16[336,640]{1,0:T(8,128)(2,1)S(1)}, bf16[336,640]{1,0:T(8,128)(2,1)S(1)}, u32[]{:S(2)}, u32[]{:S(2)}) %collective-permute-start.32) | collective-permute-done | bytes 430112 | tf_op jit(solution)/shard_map/ppermute | solution.py:52
  129.3 2.3 %fusion.80 = (bf16[1344,640]{1,0:T(8,128)(2,1)S(1)}, f32[1344,640]{1,0:T(8,128)S(1)}) fusion(bf16[1344,1008]{1,0:T(8,128)(2,1)S(1)} %bitcast.63, bf16[336,640]{1,0:T(8,128)(2,1)S(1)} %get-tuple-element.13, bf16[336,640]{1,0:T(8,128)(2,1)S(1)} %collective-permute-done.33, bf16[336,640]{1,0:T(8,128)(2,1)S(1)} %collective-permute-done.32), kind=kOutput, calls=%fused_computation.108 | convolution fusion | flops 1738813440 | bytes 9160704 | tf_op jit(solution)/shard_map/dot_general | solution.py:36
  140.8 5.8 %collective-permute-start.41 = (bf16[336,640]{1,0:T(8,128)(2,1)S(1)}, bf16[336,640]{1,0:T(8,128)(2,1)S(1)}, u32[]{:S(2)}, u32[]{:S(2)}) collective-permute-start(bf16[336,640]{1,0:T(8,128)(2,1)S(1)} %get-tuple-element.26), channel_id=1, source_target_pairs={{0,48},{32,16},{1,49},{33,17},{2,50},{34,18},{3,51},{35,19},{4,52}... | collective-permute-start | bytes 1290248 | tf_op jit(solution)/shard_map/ppermute | solution.py:67
  147.6 10.8 %collective-permute-done.38 = bf16[336,640]{1,0:T(8,128)(2,1)S(1)} collective-permute-done((bf16[336,640]{1,0:T(8,128)(2,1)S(1)}, bf16[336,640]{1,0:T(8,128)(2,1)S(1)}, u32[]{:S(2)}, u32[]{:S(2)}) %collective-permute-start.38) | collective-permute-done | bytes 430112 | tf_op jit(solution)/shard_map/ppermute | solution.py:24
  (102 shorter events, 49.1 us)
Async XLA Ops:
  2.1 23.0 %collective-permute-start.9 = (bf16[336,640]{1,0:T(8,128)(2,1)}, bf16[336,640]{1,0:T(8,128)(2,1)S(1)}, u32[]{:S(2)}, u32[]{:S(2)}) collective-permute-start(bf16[336,640]{1,0:T(8,128)(2,1)} %param.1), channel_id=1, source_target_pairs={{48,0},{16,32},{49,1},{17,33},{50,2},{18,34},{51,3},{19,35},{52,4}... | collective-permute-start | bytes 1290248 | tf_op jit(solution)/shard_map/ppermute | solution.py:52
  3.4 25.5 %collective-permute-start.7 = (bf16[336,640]{1,0:T(8,128)(2,1)}, bf16[336,640]{1,0:T(8,128)(2,1)S(1)}, u32[]{:S(2)}, u32[]{:S(2)}) collective-permute-start(bf16[336,640]{1,0:T(8,128)(2,1)} %param.1), channel_id=1, source_target_pairs={{16,0},{48,16},{0,32},{32,48},{17,1},{49,17},{1,33},{33,49},{18,2}... | collective-permute-start | bytes 1290248 | tf_op jit(solution)/shard_map/ppermute | solution.py:52
  6.5 17.0 %collective-permute-start.3 = (bf16[336,640]{1,0:T(8,128)(2,1)}, bf16[336,640]{1,0:T(8,128)(2,1)S(1)}, u32[]{:S(2)}, u32[]{:S(2)}) collective-permute-start(bf16[336,640]{1,0:T(8,128)(2,1)} %param.1), channel_id=1, source_target_pairs={{0,128},{64,192},{128,0},{192,64},{1,129},{65,193},{129,1},{193,65... | collective-permute-start | bytes 1290248 | tf_op jit(solution)/shard_map/ppermute | solution.py:24
  9.1 18.3 %collective-permute-start.1 = (bf16[336,640]{1,0:T(8,128)(2,1)}, bf16[336,640]{1,0:T(8,128)(2,1)S(1)}, u32[]{:S(2)}, u32[]{:S(2)}) collective-permute-start(bf16[336,640]{1,0:T(8,128)(2,1)} %param.1), channel_id=1, source_target_pairs={{0,192},{64,0},{128,64},{192,128},{1,193},{65,1},{129,65},{193,129... | collective-permute-start | bytes 1290248 | tf_op jit(solution)/shard_map/ppermute | solution.py:24
  11.4 17.6 %collective-permute-start = (bf16[336,640]{1,0:T(8,128)(2,1)}, bf16[336,640]{1,0:T(8,128)(2,1)S(1)}, u32[]{:S(2)}, u32[]{:S(2)}) collective-permute-start(bf16[336,640]{1,0:T(8,128)(2,1)} %param.1), channel_id=1, source_target_pairs={{0,1},{1,0},{2,3},{3,2},{4,5},{5,4},{6,7},{7,6},{8,9},{9,8},{10,11... | collective-permute-start | bytes 1290248 | tf_op jit(solution)/shard_map/ppermute | solution.py:20
  37.5 14.1 %collective-permute-start.13 = (bf16[168,512]{1,0:T(8,128)(2,1)S(1)}, bf16[168,512]{1,0:T(8,128)(2,1)S(1)}, u32[]{:S(2)}, u32[]{:S(2)}) collective-permute-start(bf16[168,512]{1,0:T(8,128)(2,1)S(1)} %get-tuple-element.33), channel_id=1, source_target_pairs={{0,12},{4,8},{8,4},{12,0},{1,13},{5,9},{9,5},{13,1},{2,14},{6,10},... | collective-permute-start | bytes 516104 | tf_op jit(solution)/shard_map/ppermute | solution.py:20
  39.3 12.3 %collective-permute-start.12 = (bf16[168,512]{1,0:T(8,128)(2,1)S(1)}, bf16[168,512]{1,0:T(8,128)(2,1)S(1)}, u32[]{:S(2)}, u32[]{:S(2)}) collective-permute-start(bf16[168,512]{1,0:T(8,128)(2,1)S(1)} %get-tuple-element.34), channel_id=1, source_target_pairs={{0,8},{4,12},{8,0},{12,4},{1,9},{5,13},{9,1},{13,5},{2,10},{6,14},... | collective-permute-start | bytes 516104 | tf_op jit(solution)/shard_map/ppermute | solution.py:20
  43.4 13.7 %collective-permute-start.22 = (bf16[168,496]{1,0:T(8,128)(2,1)S(1)}, bf16[168,496]{1,0:T(8,128)(2,1)S(1)}, u32[]{:S(2)}, u32[]{:S(2)}) collective-permute-start(bf16[168,496]{1,0:T(8,128)(2,1)S(1)} %fusion.66), channel_id=1, source_target_pairs={{0,2},{2,0},{1,3},{3,1},{4,6},{6,4},{5,7},{7,5},{8,10},{10,8},{9,1... | collective-permute-start | bytes 499976 | tf_op jit(solution)/shard_map/ppermute | solution.py:20
  51.7 12.6 %collective-permute-start.14 = (bf16[168,512]{1,0:T(8,128)(2,1)S(1)}, bf16[168,512]{1,0:T(8,128)(2,1)S(1)}, u32[]{:S(2)}, u32[]{:S(2)}) collective-permute-start(bf16[168,512]{1,0:T(8,128)(2,1)S(1)} %fusion.65), channel_id=1, source_target_pairs={{0,2},{2,0},{1,3},{3,1},{4,6},{6,4},{5,7},{7,5},{8,10},{10,8},{9,1... | collective-permute-start | bytes 516104 | tf_op jit(solution)/shard_map/ppermute | solution.py:20
  57.3 20.6 %collective-permute-start.24 = (bf16[168,496]{1,0:T(8,128)(2,1)S(1)}, bf16[168,496]{1,0:T(8,128)(2,1)S(1)}, u32[]{:S(2)}, u32[]{:S(2)}) collective-permute-start(bf16[168,496]{1,0:T(8,128)(2,1)S(1)} %get-tuple-element.16), channel_id=1, source_target_pairs={{0,8},{4,12},{8,0},{12,4},{1,9},{5,13},{9,1},{13,5},{2,10},{6,14},... | collective-permute-start | bytes 499976 | tf_op jit(solution)/shard_map/ppermute | solution.py:20
  58.7 19.2 %collective-permute-start.25 = (bf16[168,496]{1,0:T(8,128)(2,1)S(1)}, bf16[168,496]{1,0:T(8,128)(2,1)S(1)}, u32[]{:S(2)}, u32[]{:S(2)}) collective-permute-start(bf16[168,496]{1,0:T(8,128)(2,1)S(1)} %get-tuple-element.16), channel_id=1, source_target_pairs={{0,12},{4,8},{8,4},{12,0},{1,13},{5,9},{9,5},{13,1},{2,14},{6,10},... | collective-permute-start | bytes 499976 | tf_op jit(solution)/shard_map/ppermute | solution.py:20
  85.0 12.4 %collective-permute-start.27 = (bf16[336,640]{1,0:T(8,128)(2,1)S(1)}, bf16[336,640]{1,0:T(8,128)(2,1)S(1)}, u32[]{:S(2)}, u32[]{:S(2)}) collective-permute-start(bf16[336,640]{1,0:T(8,128)(2,1)S(1)} %get-tuple-element.22), channel_id=1, source_target_pairs={{0,64},{64,128},{128,192},{192,0},{1,65},{65,129},{129,193},{193,1... | collective-permute-start | bytes 1290248 | tf_op jit(solution)/shard_map/ppermute | solution.py:24
  87.7 19.7 %collective-permute-start.28 = (bf16[336,640]{1,0:T(8,128)(2,1)S(1)}, bf16[336,640]{1,0:T(8,128)(2,1)S(1)}, u32[]{:S(2)}, u32[]{:S(2)}) collective-permute-start(bf16[336,640]{1,0:T(8,128)(2,1)S(1)} %get-tuple-element.24), channel_id=1, source_target_pairs={{0,128},{64,192},{128,0},{192,64},{1,129},{65,193},{129,1},{193,65... | collective-permute-start | bytes 1290248 | tf_op jit(solution)/shard_map/ppermute | solution.py:24
  89.4 18.0 %collective-permute-start.30 = (bf16[336,640]{1,0:T(8,128)(2,1)S(1)}, bf16[336,640]{1,0:T(8,128)(2,1)S(1)}, u32[]{:S(2)}, u32[]{:S(2)}) collective-permute-start(bf16[336,640]{1,0:T(8,128)(2,1)S(1)} %get-tuple-element.27), channel_id=1, source_target_pairs={{0,16},{16,48},{32,0},{48,32},{1,17},{17,49},{33,1},{49,33},{2,18}... | collective-permute-start | bytes 1290248 | tf_op jit(solution)/shard_map/ppermute | solution.py:66
  89.8 17.7 %collective-permute-start.31 = (bf16[336,640]{1,0:T(8,128)(2,1)S(1)}, bf16[336,640]{1,0:T(8,128)(2,1)S(1)}, u32[]{:S(2)}, u32[]{:S(2)}) collective-permute-start(bf16[336,640]{1,0:T(8,128)(2,1)S(1)} %get-tuple-element.28), channel_id=1, source_target_pairs={{0,48},{32,16},{1,49},{33,17},{2,50},{34,18},{3,51},{35,19},{4,52}... | collective-permute-start | bytes 1290248 | tf_op jit(solution)/shard_map/ppermute | solution.py:67
  107.8 14.7 %collective-permute-start.33 = (bf16[336,640]{1,0:T(8,128)(2,1)S(1)}, bf16[336,640]{1,0:T(8,128)(2,1)S(1)}, u32[]{:S(2)}, u32[]{:S(2)}) collective-permute-start(bf16[336,640]{1,0:T(8,128)(2,1)S(1)} %get-tuple-element.13), channel_id=1, source_target_pairs={{48,0},{16,32},{49,1},{17,33},{50,2},{18,34},{51,3},{19,35},{52,4}... | collective-permute-start | bytes 1290248 | tf_op jit(solution)/shard_map/ppermute | solution.py:52
  109.1 20.1 %collective-permute-start.32 = (bf16[336,640]{1,0:T(8,128)(2,1)S(1)}, bf16[336,640]{1,0:T(8,128)(2,1)S(1)}, u32[]{:S(2)}, u32[]{:S(2)}) collective-permute-start(bf16[336,640]{1,0:T(8,128)(2,1)S(1)} %get-tuple-element.13), channel_id=1, source_target_pairs={{16,0},{48,16},{0,32},{32,48},{17,1},{49,17},{1,33},{33,49},{18,2}... | collective-permute-start | bytes 1290248 | tf_op jit(solution)/shard_map/ppermute | solution.py:52
  111.2 20.4 %collective-permute-start.36 = (bf16[336,640]{1,0:T(8,128)(2,1)S(1)}, bf16[336,640]{1,0:T(8,128)(2,1)S(1)}, u32[]{:S(2)}, u32[]{:S(2)}) collective-permute-start(bf16[336,640]{1,0:T(8,128)(2,1)S(1)} %get-tuple-element.13), channel_id=1, source_target_pairs={{0,64},{64,128},{128,192},{192,0},{1,65},{65,129},{129,193},{193,1... | collective-permute-start | bytes 1290248 | tf_op jit(solution)/shard_map/ppermute | solution.py:24
  111.7 19.9 %collective-permute-start.35 = (bf16[336,640]{1,0:T(8,128)(2,1)S(1)}, bf16[336,640]{1,0:T(8,128)(2,1)S(1)}, u32[]{:S(2)}, u32[]{:S(2)}) collective-permute-start(bf16[336,640]{1,0:T(8,128)(2,1)S(1)} %get-tuple-element.13), channel_id=1, source_target_pairs={{0,128},{64,192},{128,0},{192,64},{1,129},{65,193},{129,1},{193,65... | collective-permute-start | bytes 1290248 | tf_op jit(solution)/shard_map/ppermute | solution.py:24
  113.8 19.2 %collective-permute-start.34 = (bf16[336,640]{1,0:T(8,128)(2,1)S(1)}, bf16[336,640]{1,0:T(8,128)(2,1)S(1)}, u32[]{:S(2)}, u32[]{:S(2)}) collective-permute-start(bf16[336,640]{1,0:T(8,128)(2,1)S(1)} %get-tuple-element.13), channel_id=1, source_target_pairs={{0,192},{64,0},{128,64},{192,128},{1,193},{65,1},{129,65},{193,129... | collective-permute-start | bytes 1290248 | tf_op jit(solution)/shard_map/ppermute | solution.py:24
  134.9 12.6 %collective-permute-start.37 = (bf16[336,640]{1,0:T(8,128)(2,1)S(1)}, bf16[336,640]{1,0:T(8,128)(2,1)S(1)}, u32[]{:S(2)}, u32[]{:S(2)}) collective-permute-start(bf16[336,640]{1,0:T(8,128)(2,1)S(1)} %get-tuple-element.19), channel_id=1, source_target_pairs={{0,64},{64,128},{128,192},{192,0},{1,65},{65,129},{129,193},{193,1... | collective-permute-start | bytes 1290248 | tf_op jit(solution)/shard_map/ppermute | solution.py:24
  138.5 19.8 %collective-permute-start.38 = (bf16[336,640]{1,0:T(8,128)(2,1)S(1)}, bf16[336,640]{1,0:T(8,128)(2,1)S(1)}, u32[]{:S(2)}, u32[]{:S(2)}) collective-permute-start(bf16[336,640]{1,0:T(8,128)(2,1)S(1)} %get-tuple-element.21), channel_id=1, source_target_pairs={{0,128},{64,192},{128,0},{192,64},{1,129},{65,193},{129,1},{193,65... | collective-permute-start | bytes 1290248 | tf_op jit(solution)/shard_map/ppermute | solution.py:24
  139.7 18.7 %collective-permute-start.40 = (bf16[336,640]{1,0:T(8,128)(2,1)S(1)}, bf16[336,640]{1,0:T(8,128)(2,1)S(1)}, u32[]{:S(2)}, u32[]{:S(2)}) collective-permute-start(bf16[336,640]{1,0:T(8,128)(2,1)S(1)} %get-tuple-element.25), channel_id=1, source_target_pairs={{0,16},{16,48},{32,0},{48,32},{1,17},{17,49},{33,1},{49,33},{2,18}... | collective-permute-start | bytes 1290248 | tf_op jit(solution)/shard_map/ppermute | solution.py:66
  140.8 17.6 %collective-permute-start.41 = (bf16[336,640]{1,0:T(8,128)(2,1)S(1)}, bf16[336,640]{1,0:T(8,128)(2,1)S(1)}, u32[]{:S(2)}, u32[]{:S(2)}) collective-permute-start(bf16[336,640]{1,0:T(8,128)(2,1)S(1)} %get-tuple-element.26), channel_id=1, source_target_pairs={{0,48},{32,16},{1,49},{33,17},{2,50},{34,18},{3,51},{35,19},{4,52}... | collective-permute-start | bytes 1290248 | tf_op jit(solution)/shard_map/ppermute | solution.py:67
  (19 other events, 139.3 us)

commit v2 on v1

--- a/solution.py
+++ b/solution.py
@@ -56,15 +56,18 @@
     return [send_up(v, "y", 4, -s) for s in OFFSETS]
 
 
-def apply_gram(gram, columns, rows):
-    part = dot(gram, columns, 1, 0)
-    back = narrow(dot(gram[:, : 2 * B], rows, 0, 0))
-    sent, back = lax.optimization_barrier((narrow(part), back))
+def products(grams, columns, rows):
+    part = dot(grams[0], columns[0], 1, 0) + dot(grams[1], columns[1], 1, 0)
+    backs = [narrow(dot(gram[:, :B], rows, 0, 0)) for gram in grams]
+    return part, backs
+
+
+def collect(part, sent, backs):
     total = part[:B]
     for s in OFFSETS:
         total = total + wide(send_up(sent[s * B : (s + 1) * B], "y", 4, s))
-    total = total + wide(lax.ppermute(back[:B], "zl", [(b, a) for a, b in SLOT_A]))
-    total = total + wide(lax.ppermute(back[B:], "zl", [(b, a) for a, b in SLOT_B]))
+    for back, slot in zip(backs, (SLOT_A, SLOT_B)):
+        total = total + wide(lax.ppermute(back, "zl", [(b, a) for a, b in slot]))
     return total
 
 
@@ -105,20 +108,32 @@
         return narrow(dot(rows, columns, 1, 1)).reshape(4, H, columns.shape[0])
 
     cut = CUT - B
-    sum_a = sum_x(chip_chunk([za_w, zb_w[:cut]]), xi)
-    sum_b = sum_x(chip_chunk([zb_w[cut:], own_w]), xi)
-    gram = jnp.zeros((4, 2, H, 3 * B), jnp.bfloat16)
-    for total, place in ((sum_a, 0), (sum_b, CUT)):
+    sums = [
+        sum_x(chip_chunk([za_w, own_w[:cut]]), xi),
+        sum_x(chip_chunk([zb_w, own_w[cut:]]), xi),
+    ]
+    grams = []
+    for total in sums:
         part, other = gram_chunk(total, xi)
-        gram = lax.dynamic_update_slice(gram, part[:, None], (0, core, 0, place))
-        gram = lax.dynamic_update_slice(gram, other[:, None], (0, 1 - core, 0, place))
-    gram = gram.reshape(4 * B, 3 * B)
-    columns = jnp.concatenate([za, zb, momentum], axis=0)
-    first = apply_gram(gram, columns, jnp.concatenate([momentum] + y, axis=0))
-    sent = narrow(first)
-    rows = jnp.concatenate([sent] + fetch_y(sent), axis=0)
-    columns = jnp.concatenate(fetch_z(sent) + [sent], axis=0)
-    second = apply_gram(gram, columns, rows)
+        n = part.shape[2]
+        gram = jnp.zeros((4, 2, H, n), jnp.bfloat16)
+        gram = lax.dynamic_update_slice(gram, part[:, None], (0, core, 0, 0))
+        gram = lax.dynamic_update_slice(gram, other[:, None], (0, 1 - core, 0, 0))
+        grams.append(gram.reshape(4 * B, n))
+
+    def split(a, b, own):
+        return [jnp.concatenate(v, axis=0) for v in ([a, own[:cut]], [b, own[cut:]])]
+
+    part, backs = products(
+        grams, split(za, zb, momentum), jnp.concatenate([momentum] + y, axis=0)
+    )
+    sent, back_a = lax.optimization_barrier((narrow(part), backs[0]))
+    first = collect(part, sent, [back_a, backs[1]])
+    here = narrow(first)
+    rows = jnp.concatenate([here] + fetch_y(here), axis=0)
+    part, backs = products(grams, split(*fetch_z(here), here), rows)
+    sent, *backs = lax.optimization_barrier((narrow(part), *backs))
+    second = collect(part, sent, backs)
     return narrow(coef_a * wide(momentum) + coef_b * first + coef_c * second)
 
 

time: 162 us -> 175 us (1.080)
  local copies, waits for them, and re-layouts: 1.51 us -> 6.84 us
  other arithmetic: 3.32 us -> 7.1 us
  waiting for transfers between devices: 69.3 us -> 72.9 us
  matrix products: 10.5 us -> 13.2 us
  starting transfers between devices: 74.6 us -> 72.7 us
    ppermute x12, waiting for transfers between devices: 36.8 us -> 59.2 us  [send_up(): return lax.ppermute(v, axis, [(i, (i + k) % size) for i in range(size)])]
    ppermute x4, waiting for transfers between devices: 14.8 us -> 0.01 us  [fetch_z(): return [lax.ppermute(v, 'zl', SLOT_A), lax.ppermute(v, 'zl', SLOT_B)]]
    ppermute x12, starting transfers between devices: 18.1 us -> 11.9 us  [send_up(): return lax.ppermute(v, axis, [(i, (i + k) % size) for i in range(size)])]
    ppermute x22, starting transfers between devices: 36.4 us -> 41.5 us  [send_xor(): return lax.ppermute(v, axis, [(i, i ^ k) for i in range(size)])]
    ppermute x22, waiting for transfers between devices: 17.7 us -> 12.9 us  [send_xor(): return lax.ppermute(v, axis, [(i, i ^ k) for i in range(size)])]
    select_n x5, other arithmetic: 1.21 us -> 5 us  [pick(): return jnp.where(core == 0, v[:H], v[H:])]
    unnamed x3 -> x11, local copies, waits for them, and re-layouts: 0.05 us -> 3.21 us
    dot_general x6 -> x10, matrix products: 10.5 us -> 13.2 us  [dot(): lax.dot_general(a, b, (((da,), (db,)), ((), ())), preferred_element_type=...]
  transfers between devices with their start and end apart: 42 -> 42, of which waited for: 19 -> 13; matrix products, arithmetic and copies ran while one was open for 5% -> 14% of each run, Pallas kernels for 0% -> 0%
where the time goes in v2:
time: 175 us; the launch traced here: 173 us
  waiting for transfers between devices  72.9 us (42%)
  starting transfers between devices  72.7 us (42%)
  matrix products  13.2 us (8%)
  other arithmetic  7.1 us (4%)
  local copies, waits for them, and re-layouts  6.84 us (4%)
    ppermute x12, waiting for transfers between devices, send_up(): return lax.ppermute(v, axis, [(i, (i + k) % size) for i in range(size)])  59.2 us
    ppermute x22, starting transfers between devices, send_xor(): return lax.ppermute(v, axis, [(i, i ^ k) for i in range(size)])  41.5 us
    ppermute x4, starting transfers between devices, collect(): total = total + wide(lax.ppermute(back, 'zl', [(b, a) for a, b in slot]))  13.5 us
    dot_general x10, matrix products, dot(): lax.dot_general(a, b, (((da,), (db,)), ((), ())), preferred_element_type=...  13.2 us
    ppermute x22, waiting for transfers between devices, send_xor(): return lax.ppermute(v, axis, [(i, i ^ k) for i in range(size)])  12.9 us
    ppermute x12, starting transfers between devices, send_up(): return lax.ppermute(v, axis, [(i, (i + k) % size) for i in range(size)])  11.9 us
    ppermute x4, starting transfers between devices, fetch_z(): return [lax.ppermute(v, 'zl', SLOT_A), lax.ppermute(v, 'zl', SLOT_B)]  5.81 us
    select_n x5, other arithmetic, pick(): return jnp.where(core == 0, v[:H], v[H:])  5 us
  transfers between devices with their start and end apart: 42, of which 13 were waited for; matrix products, arithmetic and copies ran while one was open for 14% of the time, Pallas kernels for 0%

profile of v2, /device:TPU:1, one launch (start us, length us, event | category | flops | bytes accessed | tf_op | source)
XLA Modules:
  0.0 173.3 jit_solution(18095877180038027944)
XLA Ops:
  0.0 3.2 %collective-permute-start = (bf16[336,640]{1,0:T(8,128)(2,1)}, bf16[336,640]{1,0:T(8,128)(2,1)S(1)}, u32[]{:S(2)}, u32[]{:S(2)}) collective-permute-start(bf16[336,640]{1,0:T(8,128)(2,1)} %param.1), channel_id=1, source_target_pairs={{0,1},{1,0},{2,3},{3,2},{4,5},{5,4},{6,7},{7,6},{8,9},{9,8},{10,11... | collective-permute-start | bytes 1290248 | tf_op jit(solution)/shard_map/ppermute | solution.py:20
  5.3 3.0 %collective-permute-start.7 = (bf16[336,640]{1,0:T(8,128)(2,1)}, bf16[336,640]{1,0:T(8,128)(2,1)}, u32[]{:S(2)}, u32[]{:S(2)}) collective-permute-start(bf16[336,640]{1,0:T(8,128)(2,1)} %param.1), channel_id=1, source_target_pairs={{16,0},{48,16},{0,32},{32,48},{17,1},{49,17},{1,33},{33,49},{18,2}... | collective-permute-start | bytes 1290248 | tf_op jit(solution)/shard_map/ppermute | solution.py:52
  20.4 6.7 %collective-permute-done.5 = bf16[336,640]{1,0:T(8,128)(2,1)} collective-permute-done((bf16[336,640]{1,0:T(8,128)(2,1)}, bf16[336,640]{1,0:T(8,128)(2,1)}, u32[]{:S(2)}, u32[]{:S(2)}) %collective-permute-start.5) | collective-permute-done | bytes 430112 | tf_op jit(solution)/shard_map/ppermute | solution.py:24
  35.1 2.5 %collective-permute-start.20 = (bf16[168,496]{1,0:T(8,128)(2,1)S(1)}, bf16[168,496]{1,0:T(8,128)(2,1)S(1)}, u32[]{:S(2)}, u32[]{:S(2)}) collective-permute-start(bf16[168,496]{1,0:T(8,128)(2,1)S(1)} %get-tuple-element.32), channel_id=1, source_target_pairs={{0,8},{4,12},{8,0},{12,4},{1,9},{5,13},{9,1},{13,5},{2,10},{6,14},... | collective-permute-start | bytes 499976 | tf_op jit(solution)/shard_map/ppermute | solution.py:20
  37.8 2.1 %convolution_convert_fusion.1 = bf16[672,512]{1,0:T(8,128)(2,1)S(1)} fusion(bf16[176,1280]{1,0:T(8,128)(2,1)S(1)} %slice.120, bf16[336,640]{1,0:T(8,128)(2,1)S(1)} %collective-permute-done.8, bf16[336,640]{1,0:T(8,128)(2,1)} %collective-permute-done.7, bf16[168,640]{1,0:T(8,128)(2,1)S(1)} %collective-permute-done.6, ...), kind=kOutput, calls=%fused_computation.5 | convolution fusion | flops 898842624 | bytes 3719168 | tf_op jit(solution)/shard_map/dot_general | solution.py:36
  43.1 2.7 %collective-permute-done.20 = bf16[168,496]{1,0:T(8,128)(2,1)S(1)} collective-permute-done((bf16[168,496]{1,0:T(8,128)(2,1)S(1)}, bf16[168,496]{1,0:T(8,128)(2,1)S(1)}, u32[]{:S(2)}, u32[]{:S(2)}) %collective-permute-start.20) | collective-permute-done | bytes 166688 | tf_op jit(solution)/shard_map/ppermute | solution.py:20
  45.8 6.0 %collective-permute-done.21 = bf16[168,496]{1,0:T(8,128)(2,1)S(1)} collective-permute-done((bf16[168,496]{1,0:T(8,128)(2,1)S(1)}, bf16[168,496]{1,0:T(8,128)(2,1)S(1)}, u32[]{:S(2)}, u32[]{:S(2)}) %collective-permute-start.21) | collective-permute-done | bytes 166688 | tf_op jit(solution)/shard_map/ppermute | solution.py:20
  51.9 7.2 %collective-permute-start.22 = (bf16[168,496]{1,0:T(8,128)(2,1)S(1)}, bf16[168,496]{1,0:T(8,128)(2,1)S(1)}, u32[]{:S(2)}, u32[]{:S(2)}) collective-permute-start(bf16[168,496]{1,0:T(8,128)(2,1)S(1)} %fusion.44), channel_id=1, source_target_pairs={{0,2},{2,0},{1,3},{3,1},{4,6},{6,4},{5,7},{7,5},{8,10},{10,8},{9,1... | collective-permute-start | bytes 499976 | tf_op jit(solution)/shard_map/ppermute | solution.py:20
  59.2 3.4 %collective-permute-start.12 = (bf16[168,512]{1,0:T(8,128)(2,1)S(1)}, bf16[168,512]{1,0:T(8,128)(2,1)S(1)}, u32[]{:S(2)}, u32[]{:S(2)}) collective-permute-start(bf16[168,512]{1,0:T(8,128)(2,1)S(1)} %fusion.43), channel_id=1, source_target_pairs={{0,2},{2,0},{1,3},{3,1},{4,6},{6,4},{5,7},{7,5},{8,10},{10,8},{9,1... | collective-permute-start | bytes 516104 | tf_op jit(solution)/shard_map/ppermute | solution.py:20
  64.2 2.5 %collective-permute-start.25 = (bf16[168,496]{1,0:T(8,128)(2,1)S(1)}, bf16[168,496]{1,0:T(8,128)(2,1)S(1)}, u32[]{:S(2)}, u32[]{:S(2)}) collective-permute-start(bf16[168,496]{1,0:T(8,128)(2,1)S(1)} %get-tuple-element.20), channel_id=1, source_target_pairs={{0,12},{4,8},{8,4},{12,0},{1,13},{5,9},{9,5},{13,1},{2,14},{6,10},... | collective-permute-start | bytes 499976 | tf_op jit(solution)/shard_map/ppermute | solution.py:20
  66.7 4.2 %collective-permute-done.12 = bf16[168,512]{1,0:T(8,128)(2,1)S(1)} collective-permute-done((bf16[168,512]{1,0:T(8,128)(2,1)S(1)}, bf16[168,512]{1,0:T(8,128)(2,1)S(1)}, u32[]{:S(2)}, u32[]{:S(2)}) %collective-permute-start.12) | collective-permute-done | bytes 172064 | tf_op jit(solution)/shard_map/ppermute | solution.py:20
  72.6 2.5 %collective-permute-start.15 = (bf16[168,512]{1,0:T(8,128)(2,1)S(1)}, bf16[168,512]{1,0:T(8,128)(2,1)S(1)}, u32[]{:S(2)}, u32[]{:S(2)}) collective-permute-start(bf16[168,512]{1,0:T(8,128)(2,1)S(1)} %get-tuple-element.18), channel_id=1, source_target_pairs={{0,12},{4,8},{8,4},{12,0},{1,13},{5,9},{9,5},{13,1},{2,14},{6,10},... | collective-permute-start | bytes 516104 | tf_op jit(solution)/shard_map/ppermute | solution.py:20
  75.1 4.4 %collective-permute-start.26 = (bf16[4,168,496]{2,1,0:T(8,128)(2,1)S(1)}, bf16[4,168,496]{2,1,0:T(8,128)(2,1)S(1)}, u32[]{:S(2)}, u32[]{:S(2)}) collective-permute-start(bf16[4,168,496]{2,1,0:T(8,128)(2,1)S(1)} %bitcast_dynamic-update-slice_fusion.4), channel_id=1, source_target_pairs={{0,1},{1,0},{2,3},{3,2},{4,5},{5,4},{6,7},{7,6},{8,9},{9,8},{10,11... | collective-permute-start | bytes 1999880 | tf_op jit(solution)/shard_map/ppermute | solution.py:20
  79.8 4.0 %collective-permute-start.16 = (bf16[4,168,512]{2,1,0:T(8,128)(2,1)S(1)}, bf16[4,168,512]{2,1,0:T(8,128)(2,1)S(1)}, u32[]{:S(2)}, u32[]{:S(2)}) collective-permute-start(bf16[4,168,512]{2,1,0:T(8,128)(2,1)S(1)} %bitcast_dynamic-update-slice_fusion.8), channel_id=1, source_target_pairs={{0,1},{1,0},{2,3},{3,2},{4,5},{5,4},{6,7},{7,6},{8,9},{9,8},{10,11... | collective-permute-start | bytes 2064392 | tf_op jit(solution)/shard_map/ppermute | solution.py:20
  85.1 8.3 %collective-permute-start.31 = (bf16[336,640]{1,0:T(8,128)(2,1)S(1)}, bf16[336,640]{1,0:T(8,128)(2,1)S(1)}, u32[]{:S(2)}, u32[]{:S(2)}) collective-permute-start(bf16[336,640]{1,0:T(8,128)(2,1)S(1)} %convolution_convert_fusion.4), channel_id=1, source_target_pairs={{0,48},{32,16},{1,49},{33,17},{2,50},{34,18},{3,51},{35,19},{4,52}... | collective-permute-start | bytes 1290248 | tf_op jit(solution)/shard_map/ppermute | solution.py:70
  95.8 2.2 %fusion.57 = (bf16[1344,640]{1,0:T(8,128)(2,1)S(1)}, f32[1344,640]{1,0:T(8,128)S(1)}) fusion(f32[1344,640]{1,0:T(8,128)S(1)} %fusion.31, bf16[1344,512]{1,0:T(8,128)(2,1)S(1)} %bitcast.71, bf16[176,640]{1,0:T(8,128)(2,1)S(1)} %copy-done.1, bf16[336,640]{1,0:T(8,128)(2,1)} %collective-permute-done.7), kind=kOutput, calls=%fused_computation.104 | convolution fusion | flops 883834880 | bytes 10633216 | tf_op jit(solution)/shard_map/dot_general | solution.py:36
  98.7 3.3 %collective-permute-start.28 = (bf16[336,640]{1,0:T(8,128)(2,1)S(1)}, bf16[336,640]{1,0:T(8,128)(2,1)S(1)}, u32[]{:S(2)}, u32[]{:S(2)}) collective-permute-start(bf16[336,640]{1,0:T(8,128)(2,1)S(1)} %get-tuple-element.26), channel_id=1, source_target_pairs={{0,128},{64,192},{128,0},{192,64},{1,129},{65,193},{129,1},{193,65... | collective-permute-start | bytes 1290248 | tf_op jit(solution)/shard_map/ppermute | solution.py:24
  102.7 7.9 %collective-permute-done.27 = bf16[336,640]{1,0:T(8,128)(2,1)S(1)} collective-permute-done((bf16[336,640]{1,0:T(8,128)(2,1)S(1)}, bf16[336,640]{1,0:T(8,128)(2,1)S(1)}, u32[]{:S(2)}, u32[]{:S(2)}) %collective-permute-start.27) | collective-permute-done | bytes 430112 | tf_op jit(solution)/shard_map/ppermute | solution.py:24
  110.6 10.3 %collective-permute-done.28 = bf16[336,640]{1,0:T(8,128)(2,1)S(1)} collective-permute-done((bf16[336,640]{1,0:T(8,128)(2,1)S(1)}, bf16[336,640]{1,0:T(8,128)(2,1)S(1)}, u32[]{:S(2)}, u32[]{:S(2)}) %collective-permute-start.28) | collective-permute-done | bytes 430112 | tf_op jit(solution)/shard_map/ppermute | solution.py:24
  121.3 2.6 %collective-permute-start.34 = (bf16[336,640]{1,0:T(8,128)(2,1)S(1)}, bf16[336,640]{1,0:T(8,128)(2,1)S(1)}, u32[]{:S(2)}, u32[]{:S(2)}) collective-permute-start(bf16[336,640]{1,0:T(8,128)(2,1)S(1)} %get-tuple-element.15), channel_id=1, source_target_pairs={{0,192},{64,0},{128,64},{192,128},{1,193},{65,1},{129,65},{193,129... | collective-permute-start | bytes 1290248 | tf_op jit(solution)/shard_map/ppermute | solution.py:24
  126.1 8.0 %collective-permute-done.34 = bf16[336,640]{1,0:T(8,128)(2,1)S(1)} collective-permute-done((bf16[336,640]{1,0:T(8,128)(2,1)S(1)}, bf16[336,640]{1,0:T(8,128)(2,1)S(1)}, u32[]{:S(2)}, u32[]{:S(2)}) %collective-permute-start.34) | collective-permute-done | bytes 430112 | tf_op jit(solution)/shard_map/ppermute | solution.py:24
  136.1 9.7 %collective-permute-done.36 = bf16[336,640]{1,0:T(8,128)(2,1)S(1)} collective-permute-done((bf16[336,640]{1,0:T(8,128)(2,1)S(1)}, bf16[336,640]{1,0:T(8,128)(2,1)S(1)}, u32[]{:S(2)}, u32[]{:S(2)}) %collective-permute-start.36) | collective-permute-done | bytes 430112 | tf_op jit(solution)/shard_map/ppermute | solution.py:24
  153.7 4.8 %collective-permute-start.41 = (bf16[336,640]{1,0:T(8,128)(2,1)S(1)}, bf16[336,640]{1,0:T(8,128)(2,1)S(1)}, u32[]{:S(2)}, u32[]{:S(2)}) collective-permute-start(bf16[336,640]{1,0:T(8,128)(2,1)S(1)} %convolution_convert_fusion.2), channel_id=1, source_target_pairs={{0,48},{32,16},{1,49},{33,17},{2,50},{34,18},{3,51},{35,19},{4,52}... | collective-permute-start | bytes 1290248 | tf_op jit(solution)/shard_map/ppermute | solution.py:70
  158.5 13.1 %collective-permute-done.37 = bf16[336,640]{1,0:T(8,128)(2,1)S(1)} collective-permute-done((bf16[336,640]{1,0:T(8,128)(2,1)S(1)}, bf16[336,640]{1,0:T(8,128)(2,1)S(1)}, u32[]{:S(2)}, u32[]{:S(2)}) %collective-permute-start.37) | collective-permute-done | bytes 430112 | tf_op jit(solution)/shard_map/ppermute | solution.py:24
  (118 shorter events, 48.2 us)
Async XLA Ops:
  4.2 13.2 %collective-permute-start.3 = (bf16[336,640]{1,0:T(8,128)(2,1)}, bf16[336,640]{1,0:T(8,128)(2,1)}, u32[]{:S(2)}, u32[]{:S(2)}) collective-permute-start(bf16[336,640]{1,0:T(8,128)(2,1)} %param.1), channel_id=1, source_target_pairs={{0,128},{64,192},{128,0},{192,64},{1,129},{65,193},{129,1},{193,65... | collective-permute-start | bytes 1290248 | tf_op jit(solution)/shard_map/ppermute | solution.py:24
  4.6 22.5 %collective-permute-start.5 = (bf16[336,640]{1,0:T(8,128)(2,1)}, bf16[336,640]{1,0:T(8,128)(2,1)}, u32[]{:S(2)}, u32[]{:S(2)}) collective-permute-start(bf16[336,640]{1,0:T(8,128)(2,1)} %param.1), channel_id=1, source_target_pairs={{0,64},{64,128},{128,192},{192,0},{1,65},{65,129},{129,193},{193,1... | collective-permute-start | bytes 1290248 | tf_op jit(solution)/shard_map/ppermute | solution.py:24
  5.3 23.5 %collective-permute-start.7 = (bf16[336,640]{1,0:T(8,128)(2,1)}, bf16[336,640]{1,0:T(8,128)(2,1)}, u32[]{:S(2)}, u32[]{:S(2)}) collective-permute-start(bf16[336,640]{1,0:T(8,128)(2,1)} %param.1), channel_id=1, source_target_pairs={{16,0},{48,16},{0,32},{32,48},{17,1},{49,17},{1,33},{33,49},{18,2}... | collective-permute-start | bytes 1290248 | tf_op jit(solution)/shard_map/ppermute | solution.py:52
  12.6 17.4 %collective-permute-start.17 = (bf16[336,640]{1,0:T(8,128)(2,1)S(1)}, bf16[336,640]{1,0:T(8,128)(2,1)S(1)}, u32[]{:S(2)}, u32[]{:S(2)}) collective-permute-start(bf16[336,640]{1,0:T(8,128)(2,1)S(1)} %copy-done), channel_id=1, source_target_pairs={{48,0},{16,32},{49,1},{17,33},{50,2},{18,34},{51,3},{19,35},{52,4}... | collective-permute-start | bytes 1290248 | tf_op jit(solution)/shard_map/ppermute | solution.py:52
  16.2 16.4 %collective-permute-start.2 = (bf16[168,640]{1,0:T(8,128)(2,1)S(1)}, bf16[168,640]{1,0:T(8,128)(2,1)S(1)}, u32[]{:S(2)}, u32[]{:S(2)}) collective-permute-start(bf16[168,640]{1,0:T(8,128)(2,1)S(1)} %get-tuple-element.36), channel_id=1, source_target_pairs={{0,1},{1,0},{2,3},{3,2},{4,5},{5,4},{6,7},{7,6},{8,9},{9,8},{10,11... | collective-permute-start | bytes 645128 | tf_op jit(solution)/shard_map/ppermute | solution.py:20
  18.5 14.1 %collective-permute-start.4 = (bf16[168,640]{1,0:T(8,128)(2,1)S(1)}, bf16[168,640]{1,0:T(8,128)(2,1)S(1)}, u32[]{:S(2)}, u32[]{:S(2)}) collective-permute-start(bf16[168,640]{1,0:T(8,128)(2,1)S(1)} %get-tuple-element.38), channel_id=1, source_target_pairs={{0,1},{1,0},{2,3},{3,2},{4,5},{5,4},{6,7},{7,6},{8,9},{9,8},{10,11... | collective-permute-start | bytes 645128 | tf_op jit(solution)/shard_map/ppermute | solution.py:20
  37.6 14.2 %collective-permute-start.21 = (bf16[168,496]{1,0:T(8,128)(2,1)S(1)}, bf16[168,496]{1,0:T(8,128)(2,1)S(1)}, u32[]{:S(2)}, u32[]{:S(2)}) collective-permute-start(bf16[168,496]{1,0:T(8,128)(2,1)S(1)} %get-tuple-element.31), channel_id=1, source_target_pairs={{0,12},{4,8},{8,4},{12,0},{1,13},{5,9},{9,5},{13,1},{2,14},{6,10},... | collective-permute-start | bytes 499976 | tf_op jit(solution)/shard_map/ppermute | solution.py:20
  40.0 19.1 %collective-permute-start.10 = (bf16[168,512]{1,0:T(8,128)(2,1)S(1)}, bf16[168,512]{1,0:T(8,128)(2,1)S(1)}, u32[]{:S(2)}, u32[]{:S(2)}) collective-permute-start(bf16[168,512]{1,0:T(8,128)(2,1)S(1)} %get-tuple-element.29), channel_id=1, source_target_pairs={{0,8},{4,12},{8,0},{12,4},{1,9},{5,13},{9,1},{13,5},{2,10},{6,14},... | collective-permute-start | bytes 516104 | tf_op jit(solution)/shard_map/ppermute | solution.py:20
  41.6 17.5 %collective-permute-start.11 = (bf16[168,512]{1,0:T(8,128)(2,1)S(1)}, bf16[168,512]{1,0:T(8,128)(2,1)S(1)}, u32[]{:S(2)}, u32[]{:S(2)}) collective-permute-start(bf16[168,512]{1,0:T(8,128)(2,1)S(1)} %get-tuple-element.28), channel_id=1, source_target_pairs={{0,12},{4,8},{8,4},{12,0},{1,13},{5,9},{9,5},{13,1},{2,14},{6,10},... | collective-permute-start | bytes 516104 | tf_op jit(solution)/shard_map/ppermute | solution.py:20
  42.6 16.4 %collective-permute-start.9 = (bf16[168,512]{1,0:T(8,128)(2,1)S(1)}, bf16[168,512]{1,0:T(8,128)(2,1)S(1)}, u32[]{:S(2)}, u32[]{:S(2)}) collective-permute-start(bf16[168,512]{1,0:T(8,128)(2,1)S(1)} %get-tuple-element.27), channel_id=1, source_target_pairs={{0,4},{4,0},{8,12},{12,8},{1,5},{5,1},{9,13},{13,9},{2,6},{6,2},{1... | collective-permute-start | bytes 516104 | tf_op jit(solution)/shard_map/ppermute | solution.py:20
  79.8 14.8 %collective-permute-start.16 = (bf16[4,168,512]{2,1,0:T(8,128)(2,1)S(1)}, bf16[4,168,512]{2,1,0:T(8,128)(2,1)S(1)}, u32[]{:S(2)}, u32[]{:S(2)}) collective-permute-start(bf16[4,168,512]{2,1,0:T(8,128)(2,1)S(1)} %bitcast_dynamic-update-slice_fusion.8), channel_id=1, source_target_pairs={{0,1},{1,0},{2,3},{3,2},{4,5},{5,4},{6,7},{7,6},{8,9},{9,8},{10,11... | collective-permute-start | bytes 2064392 | tf_op jit(solution)/shard_map/ppermute | solution.py:20
  85.1 17.6 %collective-permute-start.31 = (bf16[336,640]{1,0:T(8,128)(2,1)S(1)}, bf16[336,640]{1,0:T(8,128)(2,1)S(1)}, u32[]{:S(2)}, u32[]{:S(2)}) collective-permute-start(bf16[336,640]{1,0:T(8,128)(2,1)S(1)} %convolution_convert_fusion.4), channel_id=1, source_target_pairs={{0,48},{32,16},{1,49},{33,17},{2,50},{34,18},{3,51},{35,19},{4,52}... | collective-permute-start | bytes 1290248 | tf_op jit(solution)/shard_map/ppermute | solution.py:70
  98.7 22.2 %collective-permute-start.28 = (bf16[336,640]{1,0:T(8,128)(2,1)S(1)}, bf16[336,640]{1,0:T(8,128)(2,1)S(1)}, u32[]{:S(2)}, u32[]{:S(2)}) collective-permute-start(bf16[336,640]{1,0:T(8,128)(2,1)S(1)} %get-tuple-element.26), channel_id=1, source_target_pairs={{0,128},{64,192},{128,0},{192,64},{1,129},{65,193},{129,1},{193,65... | collective-permute-start | bytes 1290248 | tf_op jit(solution)/shard_map/ppermute | solution.py:24
  101.9 19.0 %collective-permute-start.29 = (bf16[336,640]{1,0:T(8,128)(2,1)S(1)}, bf16[336,640]{1,0:T(8,128)(2,1)S(1)}, u32[]{:S(2)}, u32[]{:S(2)}) collective-permute-start(bf16[336,640]{1,0:T(8,128)(2,1)S(1)} %get-tuple-element.25), channel_id=1, source_target_pairs={{0,192},{64,0},{128,64},{192,128},{1,193},{65,1},{129,65},{193,129... | collective-permute-start | bytes 1290248 | tf_op jit(solution)/shard_map/ppermute | solution.py:24
  101.9 19.0 %collective-permute-start.30 = (bf16[336,640]{1,0:T(8,128)(2,1)S(1)}, bf16[336,640]{1,0:T(8,128)(2,1)S(1)}, u32[]{:S(2)}, u32[]{:S(2)}) collective-permute-start(bf16[336,640]{1,0:T(8,128)(2,1)S(1)} %convolution_convert_fusion.5), channel_id=1, source_target_pairs={{0,16},{16,48},{32,0},{48,32},{1,17},{17,49},{33,1},{49,33},{2,18}... | collective-permute-start | bytes 1290248 | tf_op jit(solution)/shard_map/ppermute | solution.py:70
  121.3 12.9 %collective-permute-start.34 = (bf16[336,640]{1,0:T(8,128)(2,1)S(1)}, bf16[336,640]{1,0:T(8,128)(2,1)S(1)}, u32[]{:S(2)}, u32[]{:S(2)}) collective-permute-start(bf16[336,640]{1,0:T(8,128)(2,1)S(1)} %get-tuple-element.15), channel_id=1, source_target_pairs={{0,192},{64,0},{128,64},{192,128},{1,193},{65,1},{129,65},{193,129... | collective-permute-start | bytes 1290248 | tf_op jit(solution)/shard_map/ppermute | solution.py:24
  123.9 21.9 %collective-permute-start.36 = (bf16[336,640]{1,0:T(8,128)(2,1)S(1)}, bf16[336,640]{1,0:T(8,128)(2,1)S(1)}, u32[]{:S(2)}, u32[]{:S(2)}) collective-permute-start(bf16[336,640]{1,0:T(8,128)(2,1)S(1)} %get-tuple-element.15), channel_id=1, source_target_pairs={{0,64},{64,128},{128,192},{192,0},{1,65},{65,129},{129,193},{193,1... | collective-permute-start | bytes 1290248 | tf_op jit(solution)/shard_map/ppermute | solution.py:24
  124.5 22.3 %collective-permute-start.33 = (bf16[336,640]{1,0:T(8,128)(2,1)S(1)}, bf16[336,640]{1,0:T(8,128)(2,1)S(1)}, u32[]{:S(2)}, u32[]{:S(2)}) collective-permute-start(bf16[336,640]{1,0:T(8,128)(2,1)S(1)} %get-tuple-element.15), channel_id=1, source_target_pairs={{48,0},{16,32},{49,1},{17,33},{50,2},{18,34},{51,3},{19,35},{52,4}... | collective-permute-start | bytes 1290248 | tf_op jit(solution)/shard_map/ppermute | solution.py:52
  125.9 23.3 %collective-permute-start.32 = (bf16[336,640]{1,0:T(8,128)(2,1)S(1)}, bf16[336,640]{1,0:T(8,128)(2,1)S(1)}, u32[]{:S(2)}, u32[]{:S(2)}) collective-permute-start(bf16[336,640]{1,0:T(8,128)(2,1)S(1)} %get-tuple-element.15), channel_id=1, source_target_pairs={{16,0},{48,16},{0,32},{32,48},{17,1},{49,17},{1,33},{33,49},{18,2}... | collective-permute-start | bytes 1290248 | tf_op jit(solution)/shard_map/ppermute | solution.py:52
  150.5 21.1 %collective-permute-start.37 = (bf16[336,640]{1,0:T(8,128)(2,1)S(1)}, bf16[336,640]{1,0:T(8,128)(2,1)S(1)}, u32[]{:S(2)}, u32[]{:S(2)}) collective-permute-start(bf16[336,640]{1,0:T(8,128)(2,1)S(1)} %get-tuple-element.21), channel_id=1, source_target_pairs={{0,64},{64,128},{128,192},{192,0},{1,65},{65,129},{129,193},{193,1... | collective-permute-start | bytes 1290248 | tf_op jit(solution)/shard_map/ppermute | solution.py:24
  150.6 21.0 %collective-permute-start.38 = (bf16[336,640]{1,0:T(8,128)(2,1)S(1)}, bf16[336,640]{1,0:T(8,128)(2,1)S(1)}, u32[]{:S(2)}, u32[]{:S(2)}) collective-permute-start(bf16[336,640]{1,0:T(8,128)(2,1)S(1)} %get-tuple-element.23), channel_id=1, source_target_pairs={{0,128},{64,192},{128,0},{192,64},{1,129},{65,193},{129,1},{193,65... | collective-permute-start | bytes 1290248 | tf_op jit(solution)/shard_map/ppermute | solution.py:24
  151.6 20.4 %collective-permute-start.39 = (bf16[336,640]{1,0:T(8,128)(2,1)S(1)}, bf16[336,640]{1,0:T(8,128)(2,1)S(1)}, u32[]{:S(2)}, u32[]{:S(2)}) collective-permute-start(bf16[336,640]{1,0:T(8,128)(2,1)S(1)} %get-tuple-element.22), channel_id=1, source_target_pairs={{0,192},{64,0},{128,64},{192,128},{1,193},{65,1},{129,65},{193,129... | collective-permute-start | bytes 1290248 | tf_op jit(solution)/shard_map/ppermute | solution.py:24
  153.3 18.7 %collective-permute-start.40 = (bf16[336,640]{1,0:T(8,128)(2,1)S(1)}, bf16[336,640]{1,0:T(8,128)(2,1)S(1)}, u32[]{:S(2)}, u32[]{:S(2)}) collective-permute-start(bf16[336,640]{1,0:T(8,128)(2,1)S(1)} %convolution_convert_fusion.3), channel_id=1, source_target_pairs={{0,16},{16,48},{32,0},{48,32},{1,17},{17,49},{33,1},{49,33},{2,18}... | collective-permute-start | bytes 1290248 | tf_op jit(solution)/shard_map/ppermute | solution.py:70
  153.7 18.3 %collective-permute-start.41 = (bf16[336,640]{1,0:T(8,128)(2,1)S(1)}, bf16[336,640]{1,0:T(8,128)(2,1)S(1)}, u32[]{:S(2)}, u32[]{:S(2)}) collective-permute-start(bf16[336,640]{1,0:T(8,128)(2,1)S(1)} %convolution_convert_fusion.2), channel_id=1, source_target_pairs={{0,48},{32,16},{1,49},{33,17},{2,50},{34,18},{3,51},{35,19},{4,52}... | collective-permute-start | bytes 1290248 | tf_op jit(solution)/shard_map/ppermute | solution.py:70
  (22 other events, 199.4 us)

commit v3 on v1

--- a/solution.py
+++ b/solution.py
@@ -14,6 +14,7 @@
 
 AXES = ("y", "zl", "x", "zh", "core")
 OFFSETS = (1, 2, 3)
+ORDER_X = (2, 1, 3)
 
 
 def send_xor(v, axis, size, k):
@@ -56,24 +57,35 @@
     return [send_up(v, "y", 4, -s) for s in OFFSETS]
 
 
+def add(total, v):
+    return lax.optimization_barrier(total + wide(v))
+
+
 def apply_gram(gram, columns, rows):
-    part = dot(gram, columns, 1, 0)
-    back = narrow(dot(gram[:, : 2 * B], rows, 0, 0))
-    sent, back = lax.optimization_barrier((narrow(part), back))
-    total = part[:B]
-    for s in OFFSETS:
-        total = total + wide(send_up(sent[s * B : (s + 1) * B], "y", 4, s))
-    total = total + wide(lax.ppermute(back[:B], "zl", [(b, a) for a, b in SLOT_A]))
-    total = total + wide(lax.ppermute(back[B:], "zl", [(b, a) for a, b in SLOT_B]))
-    return total
+    def row_block(s):
+        return dot(gram[s * B : (s + 1) * B], columns, 1, 0)
+
+    def over_y(s):
+        return send_up(narrow(row_block(s)), "y", 4, s)
+
+    def over_z(place, slot):
+        back = dot(gram[:, place : place + B], rows, 0, 0)
+        return lax.ppermute(narrow(back), "zl", [(b, a) for a, b in slot])
+
+    total = add(row_block(0), over_y(2))
+    total = add(total, over_z(CUT, SLOT_B))
+    total = add(total, over_y(1))
+    total = add(total, over_z(0, SLOT_A))
+    return total + wide(over_y(3))
 
 
 def sum_x(chip, xi):
     total = wide(lax.dynamic_index_in_dim(chip, xi, 0, keepdims=False))
-    for k in OFFSETS:
+    got = []
+    for k in ORDER_X:
         piece = lax.dynamic_index_in_dim(chip, xi ^ k, 0, keepdims=False)
-        total = total + wide(send_xor(piece, "x", 4, k))
-    return total
+        got.append(send_xor(piece, "x", 4, k))
+    return add(add(total, got[0]), got[1]) + wide(got[2])
 
 
 def gram_chunk(total, xi):
@@ -81,7 +93,7 @@
     mine = narrow(total / C)
     rows = jnp.zeros((4,) + mine.shape, jnp.bfloat16)
     rows = lax.dynamic_update_index_in_dim(rows, mine, xi, 0)
-    for k in OFFSETS:
+    for k in ORDER_X:
         rows = lax.dynamic_update_index_in_dim(rows, send_xor(mine, "x", 4, k), xi ^ k, 0)
     return rows, swap(rows)
 
@@ -91,7 +103,8 @@
     xi = lax.axis_index("x")
     y = fetch_y(momentum)
     za, zb = fetch_z(momentum)
-    m_o = swap(momentum)
+    later, y[0] = lax.optimization_barrier((momentum, y[0]))
+    m_o = swap(later)
     rows = [jnp.concatenate([pick(core, momentum), pick(core, m_o)], axis=1)]
     rows += [jnp.concatenate([pick(core, v), swap(pick(1 - core, v))], axis=1) for v in y]
     rows = jnp.concatenate(rows, axis=0)
@@ -105,19 +118,20 @@
         return narrow(dot(rows, columns, 1, 1)).reshape(4, H, columns.shape[0])
 
     cut = CUT - B
-    sum_a = sum_x(chip_chunk([za_w, zb_w[:cut]]), xi)
-    sum_b = sum_x(chip_chunk([zb_w[cut:], own_w]), xi)
+    sum_a = sum_x(chip_chunk([za_w, own_w[:cut]]), xi)
+    sum_b = sum_x(chip_chunk([zb_w, own_w[cut:]]), xi)
     gram = jnp.zeros((4, 2, H, 3 * B), jnp.bfloat16)
     for total, place in ((sum_a, 0), (sum_b, CUT)):
         part, other = gram_chunk(total, xi)
         gram = lax.dynamic_update_slice(gram, part[:, None], (0, core, 0, place))
         gram = lax.dynamic_update_slice(gram, other[:, None], (0, 1 - core, 0, place))
     gram = gram.reshape(4 * B, 3 * B)
-    columns = jnp.concatenate([za, zb, momentum], axis=0)
+    columns = jnp.concatenate([za, momentum[:cut], zb, momentum[cut:]], axis=0)
     first = apply_gram(gram, columns, jnp.concatenate([momentum] + y, axis=0))
     sent = narrow(first)
     rows = jnp.concatenate([sent] + fetch_y(sent), axis=0)
-    columns = jnp.concatenate(fetch_z(sent) + [sent], axis=0)
+    za, zb = fetch_z(sent)
+    columns = jnp.concatenate([za, sent[:cut], zb, sent[cut:]], axis=0)
     second = apply_gram(gram, columns, rows)
     return narrow(coef_a * wide(momentum) + coef_b * first + coef_c * second)
 

time: 162 us -> 170 us (1.049)
  matrix products: 10.5 us -> 18.5 us
  local copies, waits for them, and re-layouts: 1.51 us -> 7.94 us
  starting transfers between devices: 74.6 us -> 69.2 us
  waiting for transfers between devices: 69.3 us -> 66 us
  other arithmetic: 3.32 us -> 6.2 us
    dot_general x6 -> x14, matrix products: 10.5 us -> 18.5 us  [dot(): lax.dot_general(a, b, (((da,), (db,)), ((), ())), preferred_element_type=...]
    ppermute x12, waiting for transfers between devices: 36.8 us -> 30.3 us  [send_up(): return lax.ppermute(v, axis, [(i, (i + k) % size) for i in range(size)])]
    ppermute x22, starting transfers between devices: 36.4 us -> 31.9 us  [send_xor(): return lax.ppermute(v, axis, [(i, i ^ k) for i in range(size)])]
    ppermute x4, waiting for transfers between devices: 0.01 us -> 4.37 us  [over_z(): return lax.ppermute(narrow(back), 'zl', [(b, a) for a, b in slot])]
    slice x6 -> x7, local copies, waits for them, and re-layouts: 0.44 us -> 3.63 us  [the longest x2 3.27 us: body(): columns = jnp.concatenate([za, momentum[:cut], zb, momentum[cut:]], axis=0)]
    unnamed x3 -> x11, local copies, waits for them, and re-layouts: 0.05 us -> 3.22 us
    select_n x5, other arithmetic: 1.21 us -> 3.98 us  [pick(): return jnp.where(core == 0, v[:H], v[H:])]
    ppermute x12, starting transfers between devices: 18.1 us -> 20.1 us  [send_up(): return lax.ppermute(v, axis, [(i, (i + k) % size) for i in range(size)])]
  transfers between devices with their start and end apart: 42 -> 42, of which waited for: 19 -> 21; matrix products, arithmetic and copies ran while one was open for 5% -> 17% of each run, Pallas kernels for 0% -> 0%
where the time goes in v3:
time: 170 us; the launch traced here: 168 us
  starting transfers between devices  69.2 us (41%)
  waiting for transfers between devices  66 us (39%)
  matrix products  18.5 us (11%)
  local copies, waits for them, and re-layouts  7.94 us (5%)
  other arithmetic  6.2 us (4%)
    ppermute x22, starting transfers between devices, send_xor(): return lax.ppermute(v, axis, [(i, i ^ k) for i in range(size)])  31.9 us
    ppermute x12, waiting for transfers between devices, send_up(): return lax.ppermute(v, axis, [(i, (i + k) % size) for i in range(size)])  30.3 us
    ppermute x12, starting transfers between devices, send_up(): return lax.ppermute(v, axis, [(i, (i + k) % size) for i in range(size)])  20.1 us
    dot_general x14, matrix products, dot(): lax.dot_general(a, b, (((da,), (db,)), ((), ())), preferred_element_type=...  18.5 us
    ppermute x22, waiting for transfers between devices, send_xor(): return lax.ppermute(v, axis, [(i, i ^ k) for i in range(size)])  16.4 us
    ppermute x4, waiting for transfers between devices, fetch_z(): return [lax.ppermute(v, 'zl', SLOT_A), lax.ppermute(v, 'zl', SLOT_B)]  15 us
    ppermute x4, starting transfers between devices, over_z(): return lax.ppermute(narrow(back), 'zl', [(b, a) for a, b in slot])  10.5 us
    ppermute x4, starting transfers between devices, fetch_z(): return [lax.ppermute(v, 'zl', SLOT_A), lax.ppermute(v, 'zl', SLOT_B)]  6.68 us
  transfers between devices with their start and end apart: 42, of which 21 were waited for; matrix products, arithmetic and copies ran while one was open for 17% of the time, Pallas kernels for 0%

profile of v3, /device:TPU:1, one launch (start us, length us, event | category | flops | bytes accessed | tf_op | source)
XLA Modules:
  0.0 168.4 jit_solution(8933578350234252482)
XLA Ops:
  0.0 3.6 %collective-permute-start = (bf16[336,640]{1,0:T(8,128)(2,1)}, bf16[336,640]{1,0:T(8,128)(2,1)}, u32[]{:S(2)}, u32[]{:S(2)}) collective-permute-start(bf16[336,640]{1,0:T(8,128)(2,1)} %param.1), channel_id=1, source_target_pairs={{0,192},{64,0},{128,64},{192,128},{1,193},{65,1},{129,65},{193,129... | collective-permute-start | bytes 1290248 | tf_op jit(solution)/shard_map/ppermute | solution.py:25
  5.9 3.1 %collective-permute-start.7 = (bf16[336,640]{1,0:T(8,128)(2,1)}, bf16[336,640]{1,0:T(8,128)(2,1)}, u32[]{:S(2)}, u32[]{:S(2)}) collective-permute-start(bf16[336,640]{1,0:T(8,128)(2,1)} %param.1), channel_id=1, source_target_pairs={{16,0},{48,16},{0,32},{32,48},{17,1},{49,17},{1,33},{33,49},{18,2}... | collective-permute-start | bytes 1290248 | tf_op jit(solution)/shard_map/ppermute | solution.py:53
  15.1 6.4 %collective-permute-done = bf16[336,640]{1,0:T(8,128)(2,1)} collective-permute-done((bf16[336,640]{1,0:T(8,128)(2,1)}, bf16[336,640]{1,0:T(8,128)(2,1)}, u32[]{:S(2)}, u32[]{:S(2)}) %collective-permute-start) | collective-permute-done | bytes 430112 | tf_op jit(solution)/shard_map/ppermute | solution.py:25
  34.0 2.8 %collective-permute-start.19 = (bf16[168,496]{1,0:T(8,128)(2,1)S(1)}, bf16[168,496]{1,0:T(8,128)(2,1)S(1)}, u32[]{:S(2)}, u32[]{:S(2)}) collective-permute-start(bf16[168,496]{1,0:T(8,128)(2,1)S(1)} %get-tuple-element.19), channel_id=1, source_target_pairs={{0,8},{4,12},{8,0},{12,4},{1,9},{5,13},{9,1},{13,5},{2,10},{6,14},... | collective-permute-start | bytes 499976 | tf_op jit(solution)/shard_map/ppermute | solution.py:21
  45.1 6.0 %collective-permute-start.22 = (bf16[168,496]{1,0:T(8,128)(2,1)S(1)}, bf16[168,496]{1,0:T(8,128)(2,1)S(1)}, u32[]{:S(2)}, u32[]{:S(2)}) collective-permute-start(bf16[168,496]{1,0:T(8,128)(2,1)S(1)} %fusion.16), channel_id=1, source_target_pairs={{0,2},{2,0},{1,3},{3,1},{4,6},{6,4},{5,7},{7,5},{8,10},{10,8},{9,1... | collective-permute-start | bytes 499976 | tf_op jit(solution)/shard_map/ppermute | solution.py:21
  52.9 5.8 %collective-permute-start.12 = (bf16[168,512]{1,0:T(8,128)(2,1)S(1)}, bf16[168,512]{1,0:T(8,128)(2,1)S(1)}, u32[]{:S(2)}, u32[]{:S(2)}) collective-permute-start(bf16[168,512]{1,0:T(8,128)(2,1)S(1)} %fusion.15), channel_id=1, source_target_pairs={{0,2},{2,0},{1,3},{3,1},{4,6},{6,4},{5,7},{7,5},{8,10},{10,8},{9,1... | collective-permute-start | bytes 516104 | tf_op jit(solution)/shard_map/ppermute | solution.py:21
  58.9 2.9 %collective-permute-start.23 = (bf16[168,496]{1,0:T(8,128)(2,1)S(1)}, bf16[168,496]{1,0:T(8,128)(2,1)S(1)}, u32[]{:S(2)}, u32[]{:S(2)}) collective-permute-start(bf16[168,496]{1,0:T(8,128)(2,1)S(1)} %get-tuple-element.10), channel_id=1, source_target_pairs={{0,8},{4,12},{8,0},{12,4},{1,9},{5,13},{9,1},{13,5},{2,10},{6,14},... | collective-permute-start | bytes 499976 | tf_op jit(solution)/shard_map/ppermute | solution.py:21
  62.6 3.1 %collective-permute-done.12 = bf16[168,512]{1,0:T(8,128)(2,1)S(1)} collective-permute-done((bf16[168,512]{1,0:T(8,128)(2,1)S(1)}, bf16[168,512]{1,0:T(8,128)(2,1)S(1)}, u32[]{:S(2)}, u32[]{:S(2)}) %collective-permute-start.12) | collective-permute-done | bytes 172064 | tf_op jit(solution)/shard_map/ppermute | solution.py:21
  65.8 3.2 %collective-permute-start.13 = (bf16[168,512]{1,0:T(8,128)(2,1)S(1)}, bf16[168,512]{1,0:T(8,128)(2,1)S(1)}, u32[]{:S(2)}, u32[]{:S(2)}) collective-permute-start(bf16[168,512]{1,0:T(8,128)(2,1)S(1)} %get-tuple-element.12), channel_id=1, source_target_pairs={{0,8},{4,12},{8,0},{12,4},{1,9},{5,13},{9,1},{13,5},{2,10},{6,14},... | collective-permute-start | bytes 516104 | tf_op jit(solution)/shard_map/ppermute | solution.py:21
  69.4 2.8 %collective-permute-done.13 = bf16[168,512]{1,0:T(8,128)(2,1)S(1)} collective-permute-done((bf16[168,512]{1,0:T(8,128)(2,1)S(1)}, bf16[168,512]{1,0:T(8,128)(2,1)S(1)}, u32[]{:S(2)}, u32[]{:S(2)}) %collective-permute-start.13) | collective-permute-done | bytes 172064 | tf_op jit(solution)/shard_map/ppermute | solution.py:21
  72.2 4.3 %collective-permute-done.14 = bf16[168,512]{1,0:T(8,128)(2,1)S(1)} collective-permute-done((bf16[168,512]{1,0:T(8,128)(2,1)S(1)}, bf16[168,512]{1,0:T(8,128)(2,1)S(1)}, u32[]{:S(2)}, u32[]{:S(2)}) %collective-permute-start.14) | collective-permute-done | bytes 172064 | tf_op jit(solution)/shard_map/ppermute | solution.py:21
  84.2 4.4 %collective-permute-start.28 = (bf16[336,640]{1,0:T(8,128)(2,1)S(1)}, bf16[336,640]{1,0:T(8,128)(2,1)S(1)}, u32[]{:S(2)}, u32[]{:S(2)}) collective-permute-start(bf16[336,640]{1,0:T(8,128)(2,1)S(1)} %convolution_convert_fusion.5), channel_id=1, source_target_pairs={{0,48},{32,16},{1,49},{33,17},{2,50},{34,18},{3,51},{35,19},{4,52}... | collective-permute-start | bytes 1290248 | tf_op jit(solution)/shard_map/ppermute | solution.py:73
  92.6 5.0 %collective-permute-start.29 = (bf16[336,640]{1,0:T(8,128)(2,1)S(1)}, bf16[336,640]{1,0:T(8,128)(2,1)S(1)}, u32[]{:S(2)}, u32[]{:S(2)}) collective-permute-start(bf16[336,640]{1,0:T(8,128)(2,1)S(1)} %convolution_convert_fusion.10), channel_id=1, source_target_pairs={{0,64},{64,128},{128,192},{192,0},{1,65},{65,129},{129,193},{193,1... | collective-permute-start | bytes 1290248 | tf_op jit(solution)/shard_map/ppermute | solution.py:25
  100.3 2.6 %collective-permute-done.27 = bf16[336,640]{1,0:T(8,128)(2,1)S(1)} collective-permute-done((bf16[336,640]{1,0:T(8,128)(2,1)S(1)}, bf16[336,640]{1,0:T(8,128)(2,1)S(1)}, u32[]{:S(2)}, u32[]{:S(2)}) %collective-permute-start.27) | collective-permute-done | bytes 430112 | tf_op jit(solution)/shard_map/ppermute | solution.py:25
  104.8 8.2 %collective-permute-done.29 = bf16[336,640]{1,0:T(8,128)(2,1)S(1)} collective-permute-done((bf16[336,640]{1,0:T(8,128)(2,1)S(1)}, bf16[336,640]{1,0:T(8,128)(2,1)S(1)}, u32[]{:S(2)}, u32[]{:S(2)}) %collective-permute-start.29) | collective-permute-done | bytes 430112 | tf_op jit(solution)/shard_map/ppermute | solution.py:25
  116.7 2.9 %collective-permute-start.35 = (bf16[336,640]{1,0:T(8,128)(2,1)S(1)}, bf16[336,640]{1,0:T(8,128)(2,1)S(1)}, u32[]{:S(2)}, u32[]{:S(2)}) collective-permute-start(bf16[336,640]{1,0:T(8,128)(2,1)S(1)} %fusion.14), channel_id=1, source_target_pairs={{0,192},{64,0},{128,64},{192,128},{1,193},{65,1},{129,65},{193,129... | collective-permute-start | bytes 1290248 | tf_op jit(solution)/shard_map/ppermute | solution.py:25
  121.0 3.3 %collective-permute-done.32 = bf16[336,640]{1,0:T(8,128)(2,1)S(1)} collective-permute-done((bf16[336,640]{1,0:T(8,128)(2,1)S(1)}, bf16[336,640]{1,0:T(8,128)(2,1)S(1)}, u32[]{:S(2)}, u32[]{:S(2)}) %collective-permute-start.32) | collective-permute-done | bytes 430112 | tf_op jit(solution)/shard_map/ppermute | solution.py:53
  124.3 10.1 %collective-permute-done.33 = bf16[336,640]{1,0:T(8,128)(2,1)S(1)} collective-permute-done((bf16[336,640]{1,0:T(8,128)(2,1)S(1)}, bf16[336,640]{1,0:T(8,128)(2,1)S(1)}, u32[]{:S(2)}, u32[]{:S(2)}) %collective-permute-start.33) | collective-permute-done | bytes 430112 | tf_op jit(solution)/shard_map/ppermute | solution.py:53
  135.1 3.7 %collective-permute-start.41 = (bf16[336,640]{1,0:T(8,128)(2,1)S(1)}, bf16[336,640]{1,0:T(8,128)(2,1)S(1)}, u32[]{:S(2)}, u32[]{:S(2)}) collective-permute-start(bf16[336,640]{1,0:T(8,128)(2,1)S(1)} %convolution_convert_fusion.6), channel_id=1, source_target_pairs={{0,192},{64,0},{128,64},{192,128},{1,193},{65,1},{129,65},{193,129... | collective-permute-start | bytes 1290248 | tf_op jit(solution)/shard_map/ppermute | solution.py:25
  138.8 3.3 %collective-permute-done.37 = bf16[336,640]{1,0:T(8,128)(2,1)S(1)} collective-permute-done((bf16[336,640]{1,0:T(8,128)(2,1)S(1)}, bf16[336,640]{1,0:T(8,128)(2,1)S(1)}, u32[]{:S(2)}, u32[]{:S(2)}) %collective-permute-start.37) | collective-permute-done | bytes 430112 | tf_op jit(solution)/shard_map/ppermute | solution.py:25
  147.4 4.9 %collective-permute-start.38 = (bf16[336,640]{1,0:T(8,128)(2,1)S(1)}, bf16[336,640]{1,0:T(8,128)(2,1)S(1)}, u32[]{:S(2)}, u32[]{:S(2)}) collective-permute-start(bf16[336,640]{1,0:T(8,128)(2,1)S(1)} %convolution_convert_fusion.3), channel_id=1, source_target_pairs={{0,48},{32,16},{1,49},{33,17},{2,50},{34,18},{3,51},{35,19},{4,52}... | collective-permute-start | bytes 1290248 | tf_op jit(solution)/shard_map/ppermute | solution.py:73
  153.1 4.2 %collective-permute-done.34 = bf16[336,640]{1,0:T(8,128)(2,1)S(1)} collective-permute-done((bf16[336,640]{1,0:T(8,128)(2,1)S(1)}, bf16[336,640]{1,0:T(8,128)(2,1)S(1)}, u32[]{:S(2)}, u32[]{:S(2)}) %collective-permute-start.34) | collective-permute-done | bytes 430112 | tf_op jit(solution)/shard_map/ppermute | solution.py:25
  158.0 4.4 %collective-permute-done.38 = bf16[336,640]{1,0:T(8,128)(2,1)S(1)} collective-permute-done((bf16[336,640]{1,0:T(8,128)(2,1)S(1)}, bf16[336,640]{1,0:T(8,128)(2,1)S(1)}, u32[]{:S(2)}, u32[]{:S(2)}) %collective-permute-start.38) | collective-permute-done | bytes 430112 | tf_op jit(solution)/shard_map/ppermute | solution.py:73
  162.5 4.6 %collective-permute-done.39 = bf16[336,640]{1,0:T(8,128)(2,1)S(1)} collective-permute-done((bf16[336,640]{1,0:T(8,128)(2,1)S(1)}, bf16[336,640]{1,0:T(8,128)(2,1)S(1)}, u32[]{:S(2)}, u32[]{:S(2)}) %collective-permute-start.39) | collective-permute-done | bytes 430112 | tf_op jit(solution)/shard_map/ppermute | solution.py:25
  (130 shorter events, 62.4 us)
Async XLA Ops:
  0.0 21.5 %collective-permute-start = (bf16[336,640]{1,0:T(8,128)(2,1)}, bf16[336,640]{1,0:T(8,128)(2,1)}, u32[]{:S(2)}, u32[]{:S(2)}) collective-permute-start(bf16[336,640]{1,0:T(8,128)(2,1)} %param.1), channel_id=1, source_target_pairs={{0,192},{64,0},{128,64},{192,128},{1,193},{65,1},{129,65},{193,129... | collective-permute-start | bytes 1290248 | tf_op jit(solution)/shard_map/ppermute | solution.py:25
  3.6 21.9 %collective-permute-start.3 = (bf16[336,640]{1,0:T(8,128)(2,1)}, bf16[336,640]{1,0:T(8,128)(2,1)}, u32[]{:S(2)}, u32[]{:S(2)}) collective-permute-start(bf16[336,640]{1,0:T(8,128)(2,1)} %param.1), channel_id=1, source_target_pairs={{0,128},{64,192},{128,0},{192,64},{1,129},{65,193},{129,1},{193,65... | collective-permute-start | bytes 1290248 | tf_op jit(solution)/shard_map/ppermute | solution.py:25
  3.9 23.8 %collective-permute-start.5 = (bf16[336,640]{1,0:T(8,128)(2,1)}, bf16[336,640]{1,0:T(8,128)(2,1)S(1)}, u32[]{:S(2)}, u32[]{:S(2)}) collective-permute-start(bf16[336,640]{1,0:T(8,128)(2,1)} %param.1), channel_id=1, source_target_pairs={{0,64},{64,128},{128,192},{192,0},{1,65},{65,129},{129,193},{193,1... | collective-permute-start | bytes 1290248 | tf_op jit(solution)/shard_map/ppermute | solution.py:25
  4.6 23.7 %collective-permute-start.17 = (bf16[336,640]{1,0:T(8,128)(2,1)}, bf16[336,640]{1,0:T(8,128)(2,1)}, u32[]{:S(2)}, u32[]{:S(2)}) collective-permute-start(bf16[336,640]{1,0:T(8,128)(2,1)} %param.1), channel_id=1, source_target_pairs={{48,0},{16,32},{49,1},{17,33},{50,2},{18,34},{51,3},{19,35},{52,4}... | collective-permute-start | bytes 1290248 | tf_op jit(solution)/shard_map/ppermute | solution.py:53
  5.9 24.2 %collective-permute-start.7 = (bf16[336,640]{1,0:T(8,128)(2,1)}, bf16[336,640]{1,0:T(8,128)(2,1)}, u32[]{:S(2)}, u32[]{:S(2)}) collective-permute-start(bf16[336,640]{1,0:T(8,128)(2,1)} %param.1), channel_id=1, source_target_pairs={{16,0},{48,16},{0,32},{32,48},{17,1},{49,17},{1,33},{33,49},{18,2}... | collective-permute-start | bytes 1290248 | tf_op jit(solution)/shard_map/ppermute | solution.py:53
  39.8 11.3 %collective-permute-start.9 = (bf16[168,512]{1,0:T(8,128)(2,1)S(1)}, bf16[168,512]{1,0:T(8,128)(2,1)S(1)}, u32[]{:S(2)}, u32[]{:S(2)}) collective-permute-start(bf16[168,512]{1,0:T(8,128)(2,1)S(1)} %get-tuple-element.22), channel_id=1, source_target_pairs={{0,8},{4,12},{8,0},{12,4},{1,9},{5,13},{9,1},{13,5},{2,10},{6,14},... | collective-permute-start | bytes 516104 | tf_op jit(solution)/shard_map/ppermute | solution.py:21
  45.1 13.6 %collective-permute-start.22 = (bf16[168,496]{1,0:T(8,128)(2,1)S(1)}, bf16[168,496]{1,0:T(8,128)(2,1)S(1)}, u32[]{:S(2)}, u32[]{:S(2)}) collective-permute-start(bf16[168,496]{1,0:T(8,128)(2,1)S(1)} %fusion.16), channel_id=1, source_target_pairs={{0,2},{2,0},{1,3},{3,1},{4,6},{6,4},{5,7},{7,5},{8,10},{10,8},{9,1... | collective-permute-start | bytes 499976 | tf_op jit(solution)/shard_map/ppermute | solution.py:21
  52.9 12.7 %collective-permute-start.12 = (bf16[168,512]{1,0:T(8,128)(2,1)S(1)}, bf16[168,512]{1,0:T(8,128)(2,1)S(1)}, u32[]{:S(2)}, u32[]{:S(2)}) collective-permute-start(bf16[168,512]{1,0:T(8,128)(2,1)S(1)} %fusion.15), channel_id=1, source_target_pairs={{0,2},{2,0},{1,3},{3,1},{4,6},{6,4},{5,7},{7,5},{8,10},{10,8},{9,1... | collective-permute-start | bytes 516104 | tf_op jit(solution)/shard_map/ppermute | solution.py:21
  61.8 17.2 %collective-permute-start.24 = (bf16[168,496]{1,0:T(8,128)(2,1)S(1)}, bf16[168,496]{1,0:T(8,128)(2,1)S(1)}, u32[]{:S(2)}, u32[]{:S(2)}) collective-permute-start(bf16[168,496]{1,0:T(8,128)(2,1)S(1)} %get-tuple-element.10), channel_id=1, source_target_pairs={{0,4},{4,0},{8,12},{12,8},{1,5},{5,1},{9,13},{13,9},{2,6},{6,2},{1... | collective-permute-start | bytes 499976 | tf_op jit(solution)/shard_map/ppermute | solution.py:21
  62.0 17.0 %collective-permute-start.25 = (bf16[168,496]{1,0:T(8,128)(2,1)S(1)}, bf16[168,496]{1,0:T(8,128)(2,1)S(1)}, u32[]{:S(2)}, u32[]{:S(2)}) collective-permute-start(bf16[168,496]{1,0:T(8,128)(2,1)S(1)} %get-tuple-element.10), channel_id=1, source_target_pairs={{0,12},{4,8},{8,4},{12,0},{1,13},{5,9},{9,5},{13,1},{2,14},{6,10},... | collective-permute-start | bytes 499976 | tf_op jit(solution)/shard_map/ppermute | solution.py:21
  84.2 20.6 %collective-permute-start.28 = (bf16[336,640]{1,0:T(8,128)(2,1)S(1)}, bf16[336,640]{1,0:T(8,128)(2,1)S(1)}, u32[]{:S(2)}, u32[]{:S(2)}) collective-permute-start(bf16[336,640]{1,0:T(8,128)(2,1)S(1)} %convolution_convert_fusion.5), channel_id=1, source_target_pairs={{0,48},{32,16},{1,49},{33,17},{2,50},{34,18},{3,51},{35,19},{4,52}... | collective-permute-start | bytes 1290248 | tf_op jit(solution)/shard_map/ppermute | solution.py:73
  90.4 12.4 %collective-permute-start.27 = (bf16[336,640]{1,0:T(8,128)(2,1)S(1)}, bf16[336,640]{1,0:T(8,128)(2,1)S(1)}, u32[]{:S(2)}, u32[]{:S(2)}) collective-permute-start(bf16[336,640]{1,0:T(8,128)(2,1)S(1)} %convolution_convert_fusion.11), channel_id=1, source_target_pairs={{0,128},{64,192},{128,0},{192,64},{1,129},{65,193},{129,1},{193,65... | collective-permute-start | bytes 1290248 | tf_op jit(solution)/shard_map/ppermute | solution.py:25
  92.6 20.5 %collective-permute-start.29 = (bf16[336,640]{1,0:T(8,128)(2,1)S(1)}, bf16[336,640]{1,0:T(8,128)(2,1)S(1)}, u32[]{:S(2)}, u32[]{:S(2)}) collective-permute-start(bf16[336,640]{1,0:T(8,128)(2,1)S(1)} %convolution_convert_fusion.10), channel_id=1, source_target_pairs={{0,64},{64,128},{128,192},{192,0},{1,65},{65,129},{129,193},{193,1... | collective-permute-start | bytes 1290248 | tf_op jit(solution)/shard_map/ppermute | solution.py:25
  97.6 15.6 %collective-permute-start.30 = (bf16[336,640]{1,0:T(8,128)(2,1)S(1)}, bf16[336,640]{1,0:T(8,128)(2,1)S(1)}, u32[]{:S(2)}, u32[]{:S(2)}) collective-permute-start(bf16[336,640]{1,0:T(8,128)(2,1)S(1)} %convolution_convert_fusion.4), channel_id=1, source_target_pairs={{0,16},{16,48},{32,0},{48,32},{1,17},{17,49},{33,1},{49,33},{2,18}... | collective-permute-start | bytes 1290248 | tf_op jit(solution)/shard_map/ppermute | solution.py:73
  99.4 14.8 %collective-permute-start.31 = (bf16[336,640]{1,0:T(8,128)(2,1)S(1)}, bf16[336,640]{1,0:T(8,128)(2,1)S(1)}, u32[]{:S(2)}, u32[]{:S(2)}) collective-permute-start(bf16[336,640]{1,0:T(8,128)(2,1)S(1)} %convolution_convert_fusion.9), channel_id=1, source_target_pairs={{0,192},{64,0},{128,64},{192,128},{1,193},{65,1},{129,65},{193,129... | collective-permute-start | bytes 1290248 | tf_op jit(solution)/shard_map/ppermute | solution.py:25
  115.4 19.0 %collective-permute-start.33 = (bf16[336,640]{1,0:T(8,128)(2,1)S(1)}, bf16[336,640]{1,0:T(8,128)(2,1)S(1)}, u32[]{:S(2)}, u32[]{:S(2)}) collective-permute-start(bf16[336,640]{1,0:T(8,128)(2,1)S(1)} %fusion.14), channel_id=1, source_target_pairs={{48,0},{16,32},{49,1},{17,33},{50,2},{18,34},{51,3},{19,35},{52,4}... | collective-permute-start | bytes 1290248 | tf_op jit(solution)/shard_map/ppermute | solution.py:53
  116.7 22.1 %collective-permute-start.35 = (bf16[336,640]{1,0:T(8,128)(2,1)S(1)}, bf16[336,640]{1,0:T(8,128)(2,1)S(1)}, u32[]{:S(2)}, u32[]{:S(2)}) collective-permute-start(bf16[336,640]{1,0:T(8,128)(2,1)S(1)} %fusion.14), channel_id=1, source_target_pairs={{0,192},{64,0},{128,64},{192,128},{1,193},{65,1},{129,65},{193,129... | collective-permute-start | bytes 1290248 | tf_op jit(solution)/shard_map/ppermute | solution.py:25
  119.5 19.3 %collective-permute-start.36 = (bf16[336,640]{1,0:T(8,128)(2,1)S(1)}, bf16[336,640]{1,0:T(8,128)(2,1)S(1)}, u32[]{:S(2)}, u32[]{:S(2)}) collective-permute-start(bf16[336,640]{1,0:T(8,128)(2,1)S(1)} %fusion.14), channel_id=1, source_target_pairs={{0,128},{64,192},{128,0},{192,64},{1,129},{65,193},{129,1},{193,65... | collective-permute-start | bytes 1290248 | tf_op jit(solution)/shard_map/ppermute | solution.py:25
  120.9 21.2 %collective-permute-start.37 = (bf16[336,640]{1,0:T(8,128)(2,1)S(1)}, bf16[336,640]{1,0:T(8,128)(2,1)S(1)}, u32[]{:S(2)}, u32[]{:S(2)}) collective-permute-start(bf16[336,640]{1,0:T(8,128)(2,1)S(1)} %fusion.14), channel_id=1, source_target_pairs={{0,64},{64,128},{128,192},{192,0},{1,65},{65,129},{129,193},{193,1... | collective-permute-start | bytes 1290248 | tf_op jit(solution)/shard_map/ppermute | solution.py:25
  135.1 32.2 %collective-permute-start.41 = (bf16[336,640]{1,0:T(8,128)(2,1)S(1)}, bf16[336,640]{1,0:T(8,128)(2,1)S(1)}, u32[]{:S(2)}, u32[]{:S(2)}) collective-permute-start(bf16[336,640]{1,0:T(8,128)(2,1)S(1)} %convolution_convert_fusion.6), channel_id=1, source_target_pairs={{0,192},{64,0},{128,64},{192,128},{1,193},{65,1},{129,65},{193,129... | collective-permute-start | bytes 1290248 | tf_op jit(solution)/shard_map/ppermute | solution.py:25
  143.1 24.1 %collective-permute-start.40 = (bf16[336,640]{1,0:T(8,128)(2,1)S(1)}, bf16[336,640]{1,0:T(8,128)(2,1)S(1)}, u32[]{:S(2)}, u32[]{:S(2)}) collective-permute-start(bf16[336,640]{1,0:T(8,128)(2,1)S(1)} %convolution_convert_fusion.2), channel_id=1, source_target_pairs={{0,16},{16,48},{32,0},{48,32},{1,17},{17,49},{33,1},{49,33},{2,18}... | collective-permute-start | bytes 1290248 | tf_op jit(solution)/shard_map/ppermute | solution.py:73
  145.0 12.2 %collective-permute-start.34 = (bf16[336,640]{1,0:T(8,128)(2,1)S(1)}, bf16[336,640]{1,0:T(8,128)(2,1)S(1)}, u32[]{:S(2)}, u32[]{:S(2)}) collective-permute-start(bf16[336,640]{1,0:T(8,128)(2,1)S(1)} %convolution_convert_fusion.8), channel_id=1, source_target_pairs={{0,128},{64,192},{128,0},{192,64},{1,129},{65,193},{129,1},{193,65... | collective-permute-start | bytes 1290248 | tf_op jit(solution)/shard_map/ppermute | solution.py:25
  147.4 15.0 %collective-permute-start.38 = (bf16[336,640]{1,0:T(8,128)(2,1)S(1)}, bf16[336,640]{1,0:T(8,128)(2,1)S(1)}, u32[]{:S(2)}, u32[]{:S(2)}) collective-permute-start(bf16[336,640]{1,0:T(8,128)(2,1)S(1)} %convolution_convert_fusion.3), channel_id=1, source_target_pairs={{0,48},{32,16},{1,49},{33,17},{2,50},{34,18},{3,51},{35,19},{4,52}... | collective-permute-start | bytes 1290248 | tf_op jit(solution)/shard_map/ppermute | solution.py:73
  153.0 14.1 %collective-permute-start.39 = (bf16[336,640]{1,0:T(8,128)(2,1)S(1)}, bf16[336,640]{1,0:T(8,128)(2,1)S(1)}, u32[]{:S(2)}, u32[]{:S(2)}) collective-permute-start(bf16[336,640]{1,0:T(8,128)(2,1)S(1)} %convolution_convert_fusion.7), channel_id=1, source_target_pairs={{0,64},{64,128},{128,192},{192,0},{1,65},{65,129},{129,193},{193,1... | collective-permute-start | bytes 1290248 | tf_op jit(solution)/shard_map/ppermute | solution.py:25
  (22 other events, 164.8 us)

commit v4 on v1

--- a/solution.py
+++ b/solution.py
@@ -53,17 +53,21 @@
 
 
 def fetch_y(v):
-    return [send_up(v, "y", 4, -s) for s in OFFSETS]
+    return [send_up(v, "y", 4, -s) for s in (1, 3, 2)]
 
 
-def apply_gram(gram, columns, rows):
+def transposed(gram, rows):
+    return narrow(dot(gram[:, : 2 * B], rows, 0, 0))
+
+
+def apply_gram(gram, columns, back):
     part = dot(gram, columns, 1, 0)
-    back = narrow(dot(gram[:, : 2 * B], rows, 0, 0))
     sent, back = lax.optimization_barrier((narrow(part), back))
     total = part[:B]
-    for s in OFFSETS:
-        total = total + wide(send_up(sent[s * B : (s + 1) * B], "y", 4, s))
-    total = total + wide(lax.ppermute(back[:B], "zl", [(b, a) for a, b in SLOT_A]))
+    total = lax.optimization_barrier(total + wide(send_up(sent[3 * B : 4 * B], "y", 4, 2)))
+    total = lax.optimization_barrier(total + wide(lax.ppermute(back[:B], "zl", [(b, a) for a, b in SLOT_A])))
+    total = lax.optimization_barrier(total + wide(send_up(sent[2 * B : 3 * B], "y", 4, 3)))
+    total = lax.optimization_barrier(total + wide(send_up(sent[1 * B : 2 * B], "y", 4, 1)))
     total = total + wide(lax.ppermute(back[B:], "zl", [(b, a) for a, b in SLOT_B]))
     return total
 
@@ -114,11 +118,24 @@
         gram = lax.dynamic_update_slice(gram, other[:, None], (0, 1 - core, 0, place))
     gram = gram.reshape(4 * B, 3 * B)
     columns = jnp.concatenate([za, zb, momentum], axis=0)
-    first = apply_gram(gram, columns, jnp.concatenate([momentum] + y, axis=0))
+    rows = jnp.concatenate([momentum] + y, axis=0)
+    first = apply_gram(gram, columns, transposed(gram, rows))
     sent = narrow(first)
-    rows = jnp.concatenate([sent] + fetch_y(sent), axis=0)
-    columns = jnp.concatenate(fetch_z(sent) + [sent], axis=0)
-    second = apply_gram(gram, columns, rows)
+    rows = jnp.zeros((4 * B, sent.shape[1]), jnp.bfloat16)
+    columns = jnp.zeros((3 * B, sent.shape[1]), jnp.bfloat16)
+    rows = lax.dynamic_update_slice(rows, sent, (0, 0))
+    columns = lax.dynamic_update_slice(columns, sent, (2 * B, 0))
+    rows = lax.dynamic_update_slice(rows, send_up(sent, "y", 4, -2), (3 * B, 0))
+    rows, columns = lax.optimization_barrier((rows, columns))
+    columns = lax.dynamic_update_slice(columns, lax.ppermute(sent, "zl", SLOT_A), (0 * B, 0))
+    rows, columns = lax.optimization_barrier((rows, columns))
+    rows = lax.dynamic_update_slice(rows, send_up(sent, "y", 4, -3), (2 * B, 0))
+    rows, columns = lax.optimization_barrier((rows, columns))
+    rows = lax.dynamic_update_slice(rows, send_up(sent, "y", 4, -1), (1 * B, 0))
+    back = transposed(gram, rows)
+    columns, back = lax.optimization_barrier((columns, back))
+    columns = lax.dynamic_update_slice(columns, lax.ppermute(sent, "zl", SLOT_B), (1 * B, 0))
+    second = apply_gram(gram, columns, back)
     return narrow(coef_a * wide(momentum) + coef_b * first + coef_c * second)
 
 

time: 162 us -> 159 us (0.981); the launches traced: 160 us -> 159 us
  waiting for transfers between devices: 69.3 us -> 67.6 us
    ppermute x4 -> x2, waiting for transfers between devices: 14.8 us -> 3.38 us  [fetch_z(): return [lax.ppermute(v, 'zl', SLOT_A), lax.ppermute(v, 'zl', SLOT_B)]]
    ppermute x12, waiting for transfers between devices: 36.8 us -> 43.9 us  [send_up(): return lax.ppermute(v, axis, [(i, (i + k) % size) for i in range(size)])]
    ppermute x12, starting transfers between devices: 18.1 us -> 22.1 us  [send_up(): return lax.ppermute(v, axis, [(i, (i + k) % size) for i in range(size)])]
    ppermute x4 -> x2, starting transfers between devices: 7.68 us -> 4.35 us  [fetch_z(): return [lax.ppermute(v, 'zl', SLOT_A), lax.ppermute(v, 'zl', SLOT_B)]]
    ppermute x2, waiting for transfers between devices: 0.01 us -> 3.09 us  [apply_gram(): lax.ppermute(back[:B], 'zl', [(b, a) for a, b in SLOT_A])]
    ppermute x2, starting transfers between devices: 10.9 us -> 8.83 us  [apply_gram(): lax.ppermute(back[B:], 'zl', [(b, a) for a, b in SLOT_B])]
  transfers between devices with their start and end apart: 42 -> 42, of which waited for: 19 -> 21; matrix products, arithmetic and copies ran while one was open for 5% -> 5% of each run, Pallas kernels for 0% -> 0%
where the time goes in v4:
time: 159 us
  starting transfers between devices  74.5 us (47%)
  waiting for transfers between devices  67.6 us (43%)
  matrix products  10.5 us (7%)
  other arithmetic  3.58 us (2%)
  local copies, waits for them, and re-layouts  2 us (1%)
    ppermute x12, waiting for transfers between devices, send_up(): return lax.ppermute(v, axis, [(i, (i + k) % size) for i in range(size)])  43.9 us
    ppermute x22, starting transfers between devices, send_xor(): return lax.ppermute(v, axis, [(i, i ^ k) for i in range(size)])  37.7 us
    ppermute x12, starting transfers between devices, send_up(): return lax.ppermute(v, axis, [(i, (i + k) % size) for i in range(size)])  22.1 us
    ppermute x22, waiting for transfers between devices, send_xor(): return lax.ppermute(v, axis, [(i, i ^ k) for i in range(size)])  17.2 us
    dot_general x6, matrix products, dot(): lax.dot_general(a, b, (((da,), (db,)), ((), ())), preferred_element_type=...  10.5 us
    ppermute x2, starting transfers between devices, apply_gram(): lax.ppermute(back[B:], 'zl', [(b, a) for a, b in SLOT_B])  8.83 us
    ppermute x2, starting transfers between devices, fetch_z(): return [lax.ppermute(v, 'zl', SLOT_A), lax.ppermute(v, 'zl', SLOT_B)]  4.35 us
    ppermute x2, waiting for transfers between devices, fetch_z(): return [lax.ppermute(v, 'zl', SLOT_A), lax.ppermute(v, 'zl', SLOT_B)]  3.38 us
  transfers between devices with their start and end apart: 42, of which 21 were waited for; matrix products, arithmetic and copies ran while one was open for 5% of the time, Pallas kernels for 0%

profile of v4, /device:TPU:1, one launch (start us, length us, event | category | flops | bytes accessed | tf_op | source)
XLA Modules:
  0.0 158.6 jit_solution(12662310680123876028)
XLA Ops:
  0.0 3.7 %collective-permute-start.5 = (bf16[336,640]{1,0:T(8,128)(2,1)}, bf16[336,640]{1,0:T(8,128)(2,1)S(1)}, u32[]{:S(2)}, u32[]{:S(2)}) collective-permute-start(bf16[336,640]{1,0:T(8,128)(2,1)} %param.1), channel_id=1, source_target_pairs={{0,128},{64,192},{128,0},{192,64},{1,129},{65,193},{129,1},{193,65... | collective-permute-start | bytes 1290248 | tf_op jit(solution)/shard_map/ppermute | solution.py:24
  5.0 3.1 %collective-permute-start.7 = (bf16[336,640]{1,0:T(8,128)(2,1)}, bf16[336,640]{1,0:T(8,128)(2,1)S(1)}, u32[]{:S(2)}, u32[]{:S(2)}) collective-permute-start(bf16[336,640]{1,0:T(8,128)(2,1)} %param.1), channel_id=1, source_target_pairs={{16,0},{48,16},{0,32},{32,48},{17,1},{49,17},{1,33},{33,49},{18,2}... | collective-permute-start | bytes 1290248 | tf_op jit(solution)/shard_map/ppermute | solution.py:52
  12.7 5.0 %collective-permute-start = (bf16[336,640]{1,0:T(8,128)(2,1)}, bf16[336,640]{1,0:T(8,128)(2,1)S(1)}, u32[]{:S(2)}, u32[]{:S(2)}) collective-permute-start(bf16[336,640]{1,0:T(8,128)(2,1)} %param.1), channel_id=1, source_target_pairs={{0,1},{1,0},{2,3},{3,2},{4,5},{5,4},{6,7},{7,6},{8,9},{9,8},{10,11... | collective-permute-start | bytes 1290248 | tf_op jit(solution)/shard_map/ppermute | solution.py:20
  17.7 5.4 %collective-permute-done.3 = bf16[336,640]{1,0:T(8,128)(2,1)S(1)} collective-permute-done((bf16[336,640]{1,0:T(8,128)(2,1)}, bf16[336,640]{1,0:T(8,128)(2,1)S(1)}, u32[]{:S(2)}, u32[]{:S(2)}) %collective-permute-start.3) | collective-permute-done | bytes 430112 | tf_op jit(solution)/shard_map/ppermute | solution.py:24
  25.1 3.4 %collective-permute-done.7 = bf16[336,640]{1,0:T(8,128)(2,1)S(1)} collective-permute-done((bf16[336,640]{1,0:T(8,128)(2,1)}, bf16[336,640]{1,0:T(8,128)(2,1)S(1)}, u32[]{:S(2)}, u32[]{:S(2)}) %collective-permute-start.7) | collective-permute-done | bytes 430112 | tf_op jit(solution)/shard_map/ppermute | solution.py:52
  43.3 5.2 %collective-permute-start.22 = (bf16[168,496]{1,0:T(8,128)(2,1)S(1)}, bf16[168,496]{1,0:T(8,128)(2,1)S(1)}, u32[]{:S(2)}, u32[]{:S(2)}) collective-permute-start(bf16[168,496]{1,0:T(8,128)(2,1)S(1)} %fusion.41), channel_id=1, source_target_pairs={{0,2},{2,0},{1,3},{3,1},{4,6},{6,4},{5,7},{7,5},{8,10},{10,8},{9,1... | collective-permute-start | bytes 499976 | tf_op jit(solution)/shard_map/ppermute | solution.py:20
  48.4 3.0 %collective-permute-done.13 = bf16[168,512]{1,0:T(8,128)(2,1)S(1)} collective-permute-done((bf16[168,512]{1,0:T(8,128)(2,1)S(1)}, bf16[168,512]{1,0:T(8,128)(2,1)S(1)}, u32[]{:S(2)}, u32[]{:S(2)}) %collective-permute-start.13) | collective-permute-done | bytes 172064 | tf_op jit(solution)/shard_map/ppermute | solution.py:20
  51.6 5.4 %collective-permute-start.14 = (bf16[168,512]{1,0:T(8,128)(2,1)S(1)}, bf16[168,512]{1,0:T(8,128)(2,1)S(1)}, u32[]{:S(2)}, u32[]{:S(2)}) collective-permute-start(bf16[168,512]{1,0:T(8,128)(2,1)S(1)} %fusion.40), channel_id=1, source_target_pairs={{0,2},{2,0},{1,3},{3,1},{4,6},{6,4},{5,7},{7,5},{8,10},{10,8},{9,1... | collective-permute-start | bytes 516104 | tf_op jit(solution)/shard_map/ppermute | solution.py:20
  60.5 3.8 %collective-permute-done.14 = bf16[168,512]{1,0:T(8,128)(2,1)S(1)} collective-permute-done((bf16[168,512]{1,0:T(8,128)(2,1)S(1)}, bf16[168,512]{1,0:T(8,128)(2,1)S(1)}, u32[]{:S(2)}, u32[]{:S(2)}) %collective-permute-start.14) | collective-permute-done | bytes 172064 | tf_op jit(solution)/shard_map/ppermute | solution.py:20
  67.9 4.3 %collective-permute-done.15 = bf16[168,512]{1,0:T(8,128)(2,1)S(1)} collective-permute-done((bf16[168,512]{1,0:T(8,128)(2,1)S(1)}, bf16[168,512]{1,0:T(8,128)(2,1)S(1)}, u32[]{:S(2)}, u32[]{:S(2)}) %collective-permute-start.15) | collective-permute-done | bytes 172064 | tf_op jit(solution)/shard_map/ppermute | solution.py:20
  72.3 5.3 %collective-permute-start.18 = (bf16[4,168,512]{2,1,0:T(8,128)(2,1)S(1)}, bf16[4,168,512]{2,1,0:T(8,128)(2,1)S(1)}, u32[]{:S(2)}, u32[]{:S(2)}) collective-permute-start(bf16[4,168,512]{2,1,0:T(8,128)(2,1)S(1)} %bitcast_dynamic-update-slice_fusion.8), channel_id=1, source_target_pairs={{0,1},{1,0},{2,3},{3,2},{4,5},{5,4},{6,7},{7,6},{8,9},{9,8},{10,11... | collective-permute-start | bytes 2064392 | tf_op jit(solution)/shard_map/ppermute | solution.py:20
  82.3 2.3 %fusion.50 = (bf16[1344,640]{1,0:T(8,128)(2,1)S(1)}, f32[1344,640]{1,0:T(8,128)S(1)}) fusion(bf16[1344,1008]{1,0:T(8,128)(2,1)S(1)} %bitcast.64, bf16[336,640]{1,0:T(8,128)(2,1)S(1)} %copy-done, bf16[336,640]{1,0:T(8,128)(2,1)S(1)} %collective-permute-done.9, bf16[336,640]{1,0:T(8,128)(2,1)S(1)} %collective-permute-done.7), kind=kOutput, calls=%fused_computation.94 | convolution fusion | flops 1738813440 | bytes 9160704 | tf_op jit(solution)/shard_map/dot_general | solution.py:36
  84.8 3.2 %collective-permute-start.27 = (bf16[336,640]{1,0:T(8,128)(2,1)S(1)}, bf16[336,640]{1,0:T(8,128)(2,1)S(1)}, u32[]{:S(2)}, u32[]{:S(2)}) collective-permute-start(bf16[336,640]{1,0:T(8,128)(2,1)S(1)} %get-tuple-element.38), channel_id=1, source_target_pairs={{0,128},{64,192},{128,0},{192,64},{1,129},{65,193},{129,1},{193,65... | collective-permute-start | bytes 1290248 | tf_op jit(solution)/shard_map/ppermute | solution.py:24
  88.3 2.5 %collective-permute-start.29 = (bf16[336,640]{1,0:T(8,128)(2,1)S(1)}, bf16[336,640]{1,0:T(8,128)(2,1)S(1)}, u32[]{:S(2)}, u32[]{:S(2)}) collective-permute-start(bf16[336,640]{1,0:T(8,128)(2,1)S(1)} %get-tuple-element.37), channel_id=1, source_target_pairs={{0,192},{64,0},{128,64},{192,128},{1,193},{65,1},{129,65},{193,129... | collective-permute-start | bytes 1290248 | tf_op jit(solution)/shard_map/ppermute | solution.py:24
  90.8 4.2 %collective-permute-start.31 = (bf16[336,640]{1,0:T(8,128)(2,1)S(1)}, bf16[336,640]{1,0:T(8,128)(2,1)S(1)}, u32[]{:S(2)}, u32[]{:S(2)}) collective-permute-start(bf16[336,640]{1,0:T(8,128)(2,1)S(1)} %get-tuple-element.41), channel_id=1, source_target_pairs={{0,48},{32,16},{1,49},{33,17},{2,50},{34,18},{3,51},{35,19},{4,52}... | collective-permute-start | bytes 1290248 | tf_op jit(solution)/shard_map/ppermute | solution.py:71
  95.1 2.7 %collective-permute-done.27 = bf16[336,640]{1,0:T(8,128)(2,1)S(1)} collective-permute-done((bf16[336,640]{1,0:T(8,128)(2,1)S(1)}, bf16[336,640]{1,0:T(8,128)(2,1)S(1)}, u32[]{:S(2)}, u32[]{:S(2)}) %collective-permute-start.27) | collective-permute-done | bytes 430112 | tf_op jit(solution)/shard_map/ppermute | solution.py:24
  99.9 5.2 %collective-permute-done.29 = bf16[336,640]{1,0:T(8,128)(2,1)S(1)} collective-permute-done((bf16[336,640]{1,0:T(8,128)(2,1)S(1)}, bf16[336,640]{1,0:T(8,128)(2,1)S(1)}, u32[]{:S(2)}, u32[]{:S(2)}) %collective-permute-start.29) | collective-permute-done | bytes 430112 | tf_op jit(solution)/shard_map/ppermute | solution.py:24
  105.2 2.3 %collective-permute-done.30 = bf16[336,640]{1,0:T(8,128)(2,1)S(1)} collective-permute-done((bf16[336,640]{1,0:T(8,128)(2,1)S(1)}, bf16[336,640]{1,0:T(8,128)(2,1)S(1)}, u32[]{:S(2)}, u32[]{:S(2)}) %collective-permute-start.30) | collective-permute-done | bytes 430112 | tf_op jit(solution)/shard_map/ppermute | solution.py:24
  114.2 6.1 %collective-permute-done.32 = bf16[336,640]{1,0:T(8,128)(2,1)S(1)} collective-permute-done((bf16[336,640]{1,0:T(8,128)(2,1)S(1)}, bf16[336,640]{1,0:T(8,128)(2,1)S(1)}, u32[]{:S(2)}, u32[]{:S(2)}) %collective-permute-start.32) | collective-permute-done | bytes 430112 | tf_op jit(solution)/shard_map/ppermute | solution.py:24
  120.4 9.9 %collective-permute-done.34 = bf16[336,640]{1,0:T(8,128)(2,1)S(1)} collective-permute-done((bf16[336,640]{1,0:T(8,128)(2,1)S(1)}, bf16[336,640]{1,0:T(8,128)(2,1)S(1)}, u32[]{:S(2)}, u32[]{:S(2)}) %collective-permute-start.34) | collective-permute-done | bytes 430112 | tf_op jit(solution)/shard_map/ppermute | solution.py:24
  132.3 2.3 %fusion.51 = (bf16[1344,640]{1,0:T(8,128)(2,1)S(1)}, f32[1344,640]{1,0:T(8,128)S(1)}) fusion(bf16[1344,1008]{1,0:T(8,128)(2,1)S(1)} %bitcast.66, bf16[1008,640]{1,0:T(8,128)(2,1)S(1)} %constant_dynamic-update-slice_fusion), kind=kOutput, calls=%fused_computation.95 | convolution fusion | flops 1734942720 | bytes 9160704 | tf_op jit(solution)/shard_map/dot_general | solution.py:36
  139.9 4.6 %collective-permute-start.41 = (bf16[336,640]{1,0:T(8,128)(2,1)S(1)}, bf16[336,640]{1,0:T(8,128)(2,1)S(1)}, u32[]{:S(2)}, u32[]{:S(2)}) collective-permute-start(bf16[336,640]{1,0:T(8,128)(2,1)S(1)} %get-tuple-element.39), channel_id=1, source_target_pairs={{0,48},{32,16},{1,49},{33,17},{2,50},{34,18},{3,51},{35,19},{4,52}... | collective-permute-start | bytes 1290248 | tf_op jit(solution)/shard_map/ppermute | solution.py:71
  144.5 2.9 %collective-permute-done.37 = bf16[336,640]{1,0:T(8,128)(2,1)S(1)} collective-permute-done((bf16[336,640]{1,0:T(8,128)(2,1)S(1)}, bf16[336,640]{1,0:T(8,128)(2,1)S(1)}, u32[]{:S(2)}, u32[]{:S(2)}) %collective-permute-start.37) | collective-permute-done | bytes 430112 | tf_op jit(solution)/shard_map/ppermute | solution.py:24
  148.8 6.7 %collective-permute-done.39 = bf16[336,640]{1,0:T(8,128)(2,1)S(1)} collective-permute-done((bf16[336,640]{1,0:T(8,128)(2,1)S(1)}, bf16[336,640]{1,0:T(8,128)(2,1)S(1)}, u32[]{:S(2)}, u32[]{:S(2)}) %collective-permute-start.39) | collective-permute-done | bytes 430112 | tf_op jit(solution)/shard_map/ppermute | solution.py:24
  (117 shorter events, 55.6 us)
Async XLA Ops:
  0.0 12.7 %collective-permute-start.5 = (bf16[336,640]{1,0:T(8,128)(2,1)}, bf16[336,640]{1,0:T(8,128)(2,1)S(1)}, u32[]{:S(2)}, u32[]{:S(2)}) collective-permute-start(bf16[336,640]{1,0:T(8,128)(2,1)} %param.1), channel_id=1, source_target_pairs={{0,128},{64,192},{128,0},{192,64},{1,129},{65,193},{129,1},{193,65... | collective-permute-start | bytes 1290248 | tf_op jit(solution)/shard_map/ppermute | solution.py:24
  3.7 20.7 %collective-permute-start.9 = (bf16[336,640]{1,0:T(8,128)(2,1)}, bf16[336,640]{1,0:T(8,128)(2,1)S(1)}, u32[]{:S(2)}, u32[]{:S(2)}) collective-permute-start(bf16[336,640]{1,0:T(8,128)(2,1)} %param.1), channel_id=1, source_target_pairs={{48,0},{16,32},{49,1},{17,33},{50,2},{18,34},{51,3},{19,35},{52,4}... | collective-permute-start | bytes 1290248 | tf_op jit(solution)/shard_map/ppermute | solution.py:52
  5.0 23.4 %collective-permute-start.7 = (bf16[336,640]{1,0:T(8,128)(2,1)}, bf16[336,640]{1,0:T(8,128)(2,1)S(1)}, u32[]{:S(2)}, u32[]{:S(2)}) collective-permute-start(bf16[336,640]{1,0:T(8,128)(2,1)} %param.1), channel_id=1, source_target_pairs={{16,0},{48,16},{0,32},{32,48},{17,1},{49,17},{1,33},{33,49},{18,2}... | collective-permute-start | bytes 1290248 | tf_op jit(solution)/shard_map/ppermute | solution.py:52
  8.1 14.9 %collective-permute-start.3 = (bf16[336,640]{1,0:T(8,128)(2,1)}, bf16[336,640]{1,0:T(8,128)(2,1)S(1)}, u32[]{:S(2)}, u32[]{:S(2)}) collective-permute-start(bf16[336,640]{1,0:T(8,128)(2,1)} %param.1), channel_id=1, source_target_pairs={{0,64},{64,128},{128,192},{192,0},{1,65},{65,129},{129,193},{193,1... | collective-permute-start | bytes 1290248 | tf_op jit(solution)/shard_map/ppermute | solution.py:24
  8.5 16.0 %collective-permute-start.1 = (bf16[336,640]{1,0:T(8,128)(2,1)}, bf16[336,640]{1,0:T(8,128)(2,1)S(1)}, u32[]{:S(2)}, u32[]{:S(2)}) collective-permute-start(bf16[336,640]{1,0:T(8,128)(2,1)} %param.1), channel_id=1, source_target_pairs={{0,192},{64,0},{128,64},{192,128},{1,193},{65,1},{129,65},{193,129... | collective-permute-start | bytes 1290248 | tf_op jit(solution)/shard_map/ppermute | solution.py:24
  12.7 16.6 %collective-permute-start = (bf16[336,640]{1,0:T(8,128)(2,1)}, bf16[336,640]{1,0:T(8,128)(2,1)S(1)}, u32[]{:S(2)}, u32[]{:S(2)}) collective-permute-start(bf16[336,640]{1,0:T(8,128)(2,1)} %param.1), channel_id=1, source_target_pairs={{0,1},{1,0},{2,3},{3,2},{4,5},{5,4},{6,7},{7,6},{8,9},{9,8},{10,11... | collective-permute-start | bytes 1290248 | tf_op jit(solution)/shard_map/ppermute | solution.py:20
  37.4 14.1 %collective-permute-start.13 = (bf16[168,512]{1,0:T(8,128)(2,1)S(1)}, bf16[168,512]{1,0:T(8,128)(2,1)S(1)}, u32[]{:S(2)}, u32[]{:S(2)}) collective-permute-start(bf16[168,512]{1,0:T(8,128)(2,1)S(1)} %get-tuple-element.47), channel_id=1, source_target_pairs={{0,12},{4,8},{8,4},{12,0},{1,13},{5,9},{9,5},{13,1},{2,14},{6,10},... | collective-permute-start | bytes 516104 | tf_op jit(solution)/shard_map/ppermute | solution.py:20
  39.2 12.3 %collective-permute-start.12 = (bf16[168,512]{1,0:T(8,128)(2,1)S(1)}, bf16[168,512]{1,0:T(8,128)(2,1)S(1)}, u32[]{:S(2)}, u32[]{:S(2)}) collective-permute-start(bf16[168,512]{1,0:T(8,128)(2,1)S(1)} %get-tuple-element.48), channel_id=1, source_target_pairs={{0,8},{4,12},{8,0},{12,4},{1,9},{5,13},{9,1},{13,5},{2,10},{6,14},... | collective-permute-start | bytes 516104 | tf_op jit(solution)/shard_map/ppermute | solution.py:20
  43.3 13.7 %collective-permute-start.22 = (bf16[168,496]{1,0:T(8,128)(2,1)S(1)}, bf16[168,496]{1,0:T(8,128)(2,1)S(1)}, u32[]{:S(2)}, u32[]{:S(2)}) collective-permute-start(bf16[168,496]{1,0:T(8,128)(2,1)S(1)} %fusion.41), channel_id=1, source_target_pairs={{0,2},{2,0},{1,3},{3,1},{4,6},{6,4},{5,7},{7,5},{8,10},{10,8},{9,1... | collective-permute-start | bytes 499976 | tf_op jit(solution)/shard_map/ppermute | solution.py:20
  51.6 12.7 %collective-permute-start.14 = (bf16[168,512]{1,0:T(8,128)(2,1)S(1)}, bf16[168,512]{1,0:T(8,128)(2,1)S(1)}, u32[]{:S(2)}, u32[]{:S(2)}) collective-permute-start(bf16[168,512]{1,0:T(8,128)(2,1)S(1)} %fusion.40), channel_id=1, source_target_pairs={{0,2},{2,0},{1,3},{3,1},{4,6},{6,4},{5,7},{7,5},{8,10},{10,8},{9,1... | collective-permute-start | bytes 516104 | tf_op jit(solution)/shard_map/ppermute | solution.py:20
  57.1 20.5 %collective-permute-start.24 = (bf16[168,496]{1,0:T(8,128)(2,1)S(1)}, bf16[168,496]{1,0:T(8,128)(2,1)S(1)}, u32[]{:S(2)}, u32[]{:S(2)}) collective-permute-start(bf16[168,496]{1,0:T(8,128)(2,1)S(1)} %get-tuple-element.30), channel_id=1, source_target_pairs={{0,8},{4,12},{8,0},{12,4},{1,9},{5,13},{9,1},{13,5},{2,10},{6,14},... | collective-permute-start | bytes 499976 | tf_op jit(solution)/shard_map/ppermute | solution.py:20
  58.6 19.1 %collective-permute-start.25 = (bf16[168,496]{1,0:T(8,128)(2,1)S(1)}, bf16[168,496]{1,0:T(8,128)(2,1)S(1)}, u32[]{:S(2)}, u32[]{:S(2)}) collective-permute-start(bf16[168,496]{1,0:T(8,128)(2,1)S(1)} %get-tuple-element.30), channel_id=1, source_target_pairs={{0,12},{4,8},{8,4},{12,0},{1,13},{5,9},{9,5},{13,1},{2,14},{6,10},... | collective-permute-start | bytes 499976 | tf_op jit(solution)/shard_map/ppermute | solution.py:20
  84.8 13.0 %collective-permute-start.27 = (bf16[336,640]{1,0:T(8,128)(2,1)S(1)}, bf16[336,640]{1,0:T(8,128)(2,1)S(1)}, u32[]{:S(2)}, u32[]{:S(2)}) collective-permute-start(bf16[336,640]{1,0:T(8,128)(2,1)S(1)} %get-tuple-element.38), channel_id=1, source_target_pairs={{0,128},{64,192},{128,0},{192,64},{1,129},{65,193},{129,1},{193,65... | collective-permute-start | bytes 1290248 | tf_op jit(solution)/shard_map/ppermute | solution.py:24
  88.1 19.4 %collective-permute-start.30 = (bf16[336,640]{1,0:T(8,128)(2,1)S(1)}, bf16[336,640]{1,0:T(8,128)(2,1)S(1)}, u32[]{:S(2)}, u32[]{:S(2)}) collective-permute-start(bf16[336,640]{1,0:T(8,128)(2,1)S(1)} %get-tuple-element.36), channel_id=1, source_target_pairs={{0,64},{64,128},{128,192},{192,0},{1,65},{65,129},{129,193},{193,1... | collective-permute-start | bytes 1290248 | tf_op jit(solution)/shard_map/ppermute | solution.py:24
  88.3 16.8 %collective-permute-start.29 = (bf16[336,640]{1,0:T(8,128)(2,1)S(1)}, bf16[336,640]{1,0:T(8,128)(2,1)S(1)}, u32[]{:S(2)}, u32[]{:S(2)}) collective-permute-start(bf16[336,640]{1,0:T(8,128)(2,1)S(1)} %get-tuple-element.37), channel_id=1, source_target_pairs={{0,192},{64,0},{128,64},{192,128},{1,193},{65,1},{129,65},{193,129... | collective-permute-start | bytes 1290248 | tf_op jit(solution)/shard_map/ppermute | solution.py:24
  90.8 16.7 %collective-permute-start.31 = (bf16[336,640]{1,0:T(8,128)(2,1)S(1)}, bf16[336,640]{1,0:T(8,128)(2,1)S(1)}, u32[]{:S(2)}, u32[]{:S(2)}) collective-permute-start(bf16[336,640]{1,0:T(8,128)(2,1)S(1)} %get-tuple-element.41), channel_id=1, source_target_pairs={{0,48},{32,16},{1,49},{33,17},{2,50},{34,18},{3,51},{35,19},{4,52}... | collective-permute-start | bytes 1290248 | tf_op jit(solution)/shard_map/ppermute | solution.py:71
  107.7 12.6 %collective-permute-start.32 = (bf16[336,640]{1,0:T(8,128)(2,1)S(1)}, bf16[336,640]{1,0:T(8,128)(2,1)S(1)}, u32[]{:S(2)}, u32[]{:S(2)}) collective-permute-start(bf16[336,640]{1,0:T(8,128)(2,1)S(1)} %fusion.35), channel_id=1, source_target_pairs={{0,128},{64,192},{128,0},{192,64},{1,129},{65,193},{129,1},{193,65... | collective-permute-start | bytes 1290248 | tf_op jit(solution)/shard_map/ppermute | solution.py:24
  110.0 20.4 %collective-permute-start.34 = (bf16[336,640]{1,0:T(8,128)(2,1)S(1)}, bf16[336,640]{1,0:T(8,128)(2,1)S(1)}, u32[]{:S(2)}, u32[]{:S(2)}) collective-permute-start(bf16[336,640]{1,0:T(8,128)(2,1)S(1)} %fusion.35), channel_id=1, source_target_pairs={{0,64},{64,128},{128,192},{192,0},{1,65},{65,129},{129,193},{193,1... | collective-permute-start | bytes 1290248 | tf_op jit(solution)/shard_map/ppermute | solution.py:24
  111.0 19.4 %collective-permute-start.35 = (bf16[336,640]{1,0:T(8,128)(2,1)S(1)}, bf16[336,640]{1,0:T(8,128)(2,1)S(1)}, u32[]{:S(2)}, u32[]{:S(2)}) collective-permute-start(bf16[336,640]{1,0:T(8,128)(2,1)S(1)} %fusion.35), channel_id=1, source_target_pairs={{0,192},{64,0},{128,64},{192,128},{1,193},{65,1},{129,65},{193,129... | collective-permute-start | bytes 1290248 | tf_op jit(solution)/shard_map/ppermute | solution.py:24
  112.6 19.6 %collective-permute-start.36 = (bf16[336,640]{1,0:T(8,128)(2,1)S(1)}, bf16[336,640]{1,0:T(8,128)(2,1)S(1)}, u32[]{:S(2)}, u32[]{:S(2)}) collective-permute-start(bf16[336,640]{1,0:T(8,128)(2,1)S(1)} %fusion.35), channel_id=1, source_target_pairs={{48,0},{16,32},{49,1},{17,33},{50,2},{18,34},{51,3},{19,35},{52,4}... | collective-permute-start | bytes 1290248 | tf_op jit(solution)/shard_map/ppermute | solution.py:137
  134.8 12.6 %collective-permute-start.37 = (bf16[336,640]{1,0:T(8,128)(2,1)S(1)}, bf16[336,640]{1,0:T(8,128)(2,1)S(1)}, u32[]{:S(2)}, u32[]{:S(2)}) collective-permute-start(bf16[336,640]{1,0:T(8,128)(2,1)S(1)} %get-tuple-element.35), channel_id=1, source_target_pairs={{0,128},{64,192},{128,0},{192,64},{1,129},{65,193},{129,1},{193,65... | collective-permute-start | bytes 1290248 | tf_op jit(solution)/shard_map/ppermute | solution.py:24
  137.2 20.3 %collective-permute-start.40 = (bf16[336,640]{1,0:T(8,128)(2,1)S(1)}, bf16[336,640]{1,0:T(8,128)(2,1)S(1)}, u32[]{:S(2)}, u32[]{:S(2)}) collective-permute-start(bf16[336,640]{1,0:T(8,128)(2,1)S(1)} %get-tuple-element.33), channel_id=1, source_target_pairs={{0,64},{64,128},{128,192},{192,0},{1,65},{65,129},{129,193},{193,1... | collective-permute-start | bytes 1290248 | tf_op jit(solution)/shard_map/ppermute | solution.py:24
  138.6 16.9 %collective-permute-start.39 = (bf16[336,640]{1,0:T(8,128)(2,1)S(1)}, bf16[336,640]{1,0:T(8,128)(2,1)S(1)}, u32[]{:S(2)}, u32[]{:S(2)}) collective-permute-start(bf16[336,640]{1,0:T(8,128)(2,1)S(1)} %get-tuple-element.34), channel_id=1, source_target_pairs={{0,192},{64,0},{128,64},{192,128},{1,193},{65,1},{129,65},{193,129... | collective-permute-start | bytes 1290248 | tf_op jit(solution)/shard_map/ppermute | solution.py:24
  139.9 17.6 %collective-permute-start.41 = (bf16[336,640]{1,0:T(8,128)(2,1)S(1)}, bf16[336,640]{1,0:T(8,128)(2,1)S(1)}, u32[]{:S(2)}, u32[]{:S(2)}) collective-permute-start(bf16[336,640]{1,0:T(8,128)(2,1)S(1)} %get-tuple-element.39), channel_id=1, source_target_pairs={{0,48},{32,16},{1,49},{33,17},{2,50},{34,18},{3,51},{35,19},{4,52}... | collective-permute-start | bytes 1290248 | tf_op jit(solution)/shard_map/ppermute | solution.py:71
  (19 other events, 140.2 us)
